TPU v7x, 32 devices: a whole 2x2x4 slice. The times are simulated.
32 devices in a mesh: sub: 2 (over core), row: 4 (over y, x), col: 4 (over z).
Axes of the slice: x: 2, y: 2, z: 4, core: 2. Of those that a mesh axis runs over, the one named last changes fastest.
Arguments:
- front: float32 [16, 8, 128, 32, 4, 128], P(None, ('sub', 'row'), None, None, 'col'), may hold values from -2.4 to 7.5, as said below
- child_tiles: bfloat16 [4096, 128, 128], P(('sub', 'row', 'col')), may hold values from -2.390625 to 2.390625
- tile_owner: int32 [4096, 1], P(('sub', 'row', 'col')), may hold values from 0 to 31; in each aligned block of 128 rows (0 to 127, 128 to 255, ...) at most 8 rows name the same one
- tile_slot: int32 [4096], P(('sub', 'row', 'col')), may hold values from 2 to 511
Outputs:
- updated: float32 [16, 8, 128, 32, 4, 128], P(None, ('sub', 'row'), None, None, 'col')
- panel: bfloat16 [16, 8, 128, 2, 4, 128], P(None, ('sub', 'row'), None, None, 'col')
Inputs may be any that keep to these rules, and one draw needn't show every extreme that they name: The leading 1024 x 1024 block of front, made symmetric from its lower triangle, is positive definite. `tile_owner`: at most 8 of the tiles of one device go to one owner.
All inputs are finite; a program needn't handle non-finite values.
Results may differ from a plain program's by a relative error of at most 0.0038.
Values may be sent and summed in bfloat16 or wider, within the bound.
No kernel may reach another device: no remote copies, remote signals or barrier semaphores. Data moves between devices by JAX's collectives and lax.ppermute only.
A program may use at most 256 MiB of HBM per device.

v0:
```python
import jax
import jax.numpy as jnp
from jax import lax
from jax.sharding import PartitionSpec as P

NB = 1024


def broadcast(block, axis, source):
    block = jnp.where(lax.axis_index(axis) == source, block, jnp.zeros_like(block))
    return lax.psum(block, axis)


def local(front, child_tiles, tile_owner, tile_slot):
    row_tiles, _, tile_size, col_tiles, _, _ = front.shape
    sub_count = lax.axis_size("sub")
    row_count = lax.axis_size("row")
    col_count = lax.axis_size("col")
    dev_count = sub_count * row_count * col_count
    tile_count = child_tiles.shape[0]
    capacity = max(2, 2 * tile_count // dev_count)
    panel_tiles = NB // tile_size
    per_col = panel_tiles // col_count
    height = row_tiles * tile_size
    local_front = front.reshape(row_tiles, tile_size, col_tiles, tile_size)
    owners = tile_owner[:, 0]
    matches = (owners[:, None] == jnp.arange(dev_count, dtype=jnp.int32)[None, :]).astype(jnp.int32)
    before = jnp.cumsum(matches, 0) - matches
    placed = jnp.sum(before * matches, 1)
    outgoing = (
        jnp.zeros((dev_count, capacity, tile_size, tile_size), jnp.bfloat16)
        .at[owners, placed]
        .set(child_tiles)
    )
    targets = jnp.full((dev_count, capacity), -1, jnp.int32).at[owners, placed].set(tile_slot)
    arrived, landing = (
        lax.all_to_all(outgoing, ("sub", "row", "col"), split_axis=0, concat_axis=0, tiled=True),
        lax.all_to_all(targets, ("sub", "row", "col"), split_axis=0, concat_axis=0, tiled=True),
    )
    arrived = arrived.reshape(dev_count * capacity, tile_size, tile_size)
    landing = landing.reshape(dev_count * capacity)
    selector = (
        landing[:, None] == jnp.arange(row_tiles * col_tiles, dtype=jnp.int32)[None, :]
    ).astype(jnp.bfloat16)
    selector = selector.reshape(dev_count * capacity, row_tiles, col_tiles)
    assembled = local_front + jnp.einsum(
        "kqs,kab->qasb", selector, arrived, preferred_element_type=jnp.float32
    )
    sub_index = lax.axis_index("sub")
    row_index = lax.axis_index("row")
    col_index = lax.axis_index("col")
    group_id = sub_index * row_count + row_index
    corner = assembled[0, :, :per_col, :]
    beside_all = lax.all_gather(corner, ("row", "col"), axis=0, tiled=True)
    beside_all = beside_all.reshape(row_count, col_count, tile_size, per_col, tile_size)
    beside_all = beside_all.transpose(0, 2, 3, 1, 4).reshape(row_count * tile_size, NB)
    blocks = []
    for owner_sub in range(panel_tiles // row_count):
        blocks.append(broadcast(beside_all, "sub", owner_sub))
    pivot = jnp.concatenate(blocks, 0)
    symmetric = jnp.tril(pivot) + jnp.tril(pivot, -1).T
    factor = jnp.linalg.cholesky(symmetric)
    panel_cols = assembled[:, :, :per_col, :].reshape(height, per_col, 1, tile_size)
    widened = lax.all_gather(panel_cols, "col", axis=2, tiled=True).reshape(height, NB)
    solved = jax.scipy.linalg.solve_triangular(factor, widened.T, lower=True).T.astype(jnp.bfloat16)
    leading = lax.dynamic_slice_in_dim(
        factor, jnp.minimum(group_id, panel_tiles - 1) * tile_size, tile_size, 0
    ).astype(jnp.bfloat16)
    upper = jnp.where(group_id < panel_tiles, leading, solved[:tile_size])
    panel_rows = jnp.concatenate([upper, solved[tile_size:]], 0)
    panel_out = lax.dynamic_index_in_dim(
        panel_rows.reshape(row_tiles, tile_size, per_col, col_count, tile_size),
        col_index,
        3,
        keepdims=True,
    )
    panel_out = panel_out.reshape(row_tiles, 1, tile_size, per_col, 1, tile_size)
    across = broadcast(panel_rows, "row", col_index)
    update = jnp.einsum(
        "rk,nqbk->rqnb",
        panel_rows,
        lax.all_gather(across.reshape(1, row_tiles, tile_size, NB), "sub", axis=0, tiled=True),
        preferred_element_type=jnp.float32,
    )
    update = update.reshape(row_tiles, tile_size, col_tiles, tile_size)
    row_tile = jnp.arange(row_tiles, dtype=jnp.int32) * (row_count * sub_count) + group_id
    col_tile = jnp.arange(col_tiles, dtype=jnp.int32) * col_count + col_index
    trailing_mask = (row_tile >= panel_tiles)[:, None, None, None] & (col_tile >= panel_tiles)[
        None, None, :, None
    ]
    result = jnp.where(trailing_mask, assembled - update, assembled)
    return (result.reshape(front.shape), panel_out)


def solution(mesh):
    return jax.shard_map(
        local,
        mesh=mesh,
        in_specs=(
            P(None, ("sub", "row"), None, None, "col", None),
            P(("sub", "row", "col"), None, None),
            P(("sub", "row", "col"), None),
            P(("sub", "row", "col")),
        ),
        out_specs=(
            P(None, ("sub", "row"), None, None, "col", None),
            P(None, ("sub", "row"), None, None, "col", None),
        ),
        check_vma=False,
    )
```

profile of v0, /device:TPU:0, one launch (start us, length us, event | category | flops | bytes accessed | tf_op | source)
XLA Modules:
  0.0 1083.9 jit_solution(6952406624175272684)
XLA Ops:
  10.4 10.9 %scatter_fusion.1 = s32[32,8]{0,1:T(8,128)S(1)} fusion(s32[32,8]{0,1:T(8,128)S(1)} %broadcast_in_dim.35, s32[128]{0:T(128)S(1)} %fusion.80, s32[128]{0:T(128)} %param.7), kind=kCustom, calls=%fused_computation.1 | custom fusion | bytes 2560 | tf_op jit(solution)/shard_map/scatter | solution.py:35
  34.9 20.7 %scatter_fusion = bf16[32,8,128,128]{3,2,1,0:T(8,128)(2,1)} fusion(bf16[32,8,128,128]{3,2,1,0:T(8,128)(2,1)} %broadcast_in_dim.34, s32[128]{0:T(128)S(1)} %fusion.80, bf16[128,128,128]{2,1,0:T(8,128)(2,1)} %param.5), kind=kCustom, calls=%fused_computation | custom fusion | bytes 12583936 | tf_op jit(solution)/shard_map/scatter | solution.py:33
  62.9 179.7 %all-to-all-done = bf16[32,8,128,128]{3,2,1,0:T(8,128)(2,1)} async-done(((bf16[32,8,128,128]{3,2,1,0:T(8,128)(2,1)}), bf16[32,8,128,128]{3,2,1,0:T(8,128)(2,1)}, u32[]{:S(2)}, u32[]{:S(2)}) %all-to-all-start) | async-done | bytes 8388640 | tf_op jit(solution)/shard_map/all_to_all | solution.py:37
  242.6 34.5 %bitcast_add_fusion = f32[16,128,32,128]{3,2,0,1:T(8,128)} fusion(f32[16,1,128,32,1,128]{5,4,3,2,1,0:T(1,128)} %param.4, bf16[32,8,128,128]{3,2,1,0:T(8,128)(2,1)} %all-to-all-done, s32[16,32]{1,0:T(8,128)S(1)} %multiply_add_fusion, s32[256]{0:T(256)S(1)} %eq.54), kind=kOutput, calls=%fused_computation.6 | convolution fusion | flops 4303486976 | bytes 75500544 | tf_op jit(solution)/shard_map/kqs,kab->qasb/dot_general | solution.py:46
  279.4 63.9 %all-gather.9.cloned.1.call-done = f32[1,2048,2,128]{3,2,0,1:T(2,128)} async-done(((f32[1,128,2,128]{3,2,0,1:T(2,128)}), f32[1,2048,2,128]{3,2,0,1:T(2,128)}) %all-gather.9.cloned.1.call-update) | async-done | bytes 2097168 | tf_op jit(solution)/shard_map/all_gather | solution.py:54
  364.4 20.5 %all-reduce.7.cloned.1.call-done = (f32[512,1024]{1,0:T(8,128)}, f32[512,1024]{1,0:T(8,128)}) async-done(((f32[512,1024]{1,0:T(8,128)}, f32[512,1024]{1,0:T(8,128)}), (f32[512,1024]{1,0:T(8,128)}, f32[512,1024]{1,0:T(8,128)})) %all-reduce.7.cloned.1.call-update) | async-done | bytes 4194320 | tf_op jit(solution)/shard_map/psum | solution.py:11
  414.9 11.7 %cholesky.222 = f32[128,128]{1,0:T(8,128)S(1)} custom-call(f32[128,128]{1,0:T(8,128)S(1)} %cholesky.577), custom_call_target="Cholesky" | custom-call | tf_op jit(solution)/shard_map/jit(cholesky)/cholesky | solution.py:62
  426.6 9.8 custom-call.63
  442.9 11.9 %cholesky.243 = f32[128,128]{1,0:T(8,128)S(1)} custom-call(f32[128,128]{1,0:T(8,128)S(1)} %cholesky.581), custom_call_target="Cholesky" | custom-call | tf_op jit(solution)/shard_map/jit(cholesky)/cholesky | solution.py:62
  468.6 11.7 %cholesky.466 = f32[128,128]{1,0:T(8,128)S(1)} custom-call(f32[128,128]{1,0:T(8,128)S(1)} %cholesky.586), custom_call_target="Cholesky" | custom-call | tf_op jit(solution)/shard_map/jit(cholesky)/cholesky | solution.py:62
  494.3 12.1 %cholesky.485 = f32[128,128]{1,0:T(8,128)S(1)} custom-call(f32[128,128]{1,0:T(8,128)S(1)} %cholesky.591), custom_call_target="Cholesky" | custom-call | tf_op jit(solution)/shard_map/jit(cholesky)/cholesky | solution.py:62
  507.1 9.8 custom-call.66
  520.3 11.7 %cholesky.504 = f32[128,128]{1,0:T(8,128)S(1)} custom-call(f32[128,128]{1,0:T(8,128)S(1)} %cholesky.596), custom_call_target="Cholesky" | custom-call | tf_op jit(solution)/shard_map/jit(cholesky)/cholesky | solution.py:62
  532.7 10.0 custom-call.67
  546.0 11.7 %cholesky.524 = f32[128,128]{1,0:T(8,128)S(1)} custom-call(f32[128,128]{1,0:T(8,128)S(1)} %cholesky.601), custom_call_target="Cholesky" | custom-call | tf_op jit(solution)/shard_map/jit(cholesky)/cholesky | solution.py:62
  571.2 11.7 %cholesky.544 = f32[128,128]{1,0:T(8,128)S(1)} custom-call(f32[128,128]{1,0:T(8,128)S(1)} %cholesky.606), custom_call_target="Cholesky" | custom-call | tf_op jit(solution)/shard_map/jit(cholesky)/cholesky | solution.py:62
  595.9 11.7 %cholesky.562 = f32[128,128]{1,0:T(8,128)S(1)} custom-call(f32[128,128]{1,0:T(8,128)S(1)} %convolution_subtract_fusion.11), custom_call_target="Cholesky" | custom-call | tf_op jit(solution)/shard_map/jit(cholesky)/cholesky | solution.py:62
  622.9 22.7 %while.1 = (s32[]{:T(128)}, f32[1024,1024]{1,0:T(8,128)}, s32[8,2]{0,1:T(2,128)S(1)}, f32[8,128,128]{2,1,0:T(8,128)S(1)}, s32[]{:T(128)}) while((s32[]{:T(128)}, f32[1024,1024]{1,0:T(8,128)}, s32[8,2]{0,1:T(2,128)S(1)}, f32[8,128,128]{2,1,0:T(8,128)S(1)}, s32[]{:T(128)}) %tuple.68), condition=%wide.while_cond, body=%wide.while_body.sunk | while | flops 2 | bytes 131189 | solution.py:65
  645.7 78.6 %custom-call.70 = f32[8,128,128]{1,2,0:T(8,128)S(1)} custom-call(f32[8,128,128]{2,1,0:T(8,128)S(1)} %get-tuple-element.9), custom_call_target="InvertDiagBlocksLowerTriangular" | custom-call | tf_op jit(solution)/shard_map/jit(_solve_triangular)/triangular_solve | solution.py:65
  812.2 105.4 %all-reduce.5.cloned.1.call-done = bf16[1,16,128,1024]{3,2,1,0:T(8,128)(2,1)} async-done(((bf16[1,16,128,1024]{3,2,1,0:T(8,128)(2,1)}), bf16[1,16,128,1024]{3,2,1,0:T(8,128)(2,1)}) %all-reduce.5.cloned.1.call-update) | async-done | bytes 4194320 | tf_op jit(solution)/shard_map/psum | solution.py:11
  938.9 25.3 %convolution_bitcast_fusion = f32[2048,16,2,128]{0,3,1,2:T(8,128)} fusion(bf16[2,16,128,1024]{3,2,1,0:T(8,128)(2,1)} %all-gather.7.cloned.1.call-done, bf16[1920,1024]{1,0:T(8,128)(2,1)} %copy-done.1, bf16[128,1024]{1,0:T(8,128)(2,1)S(1)} %fusion.50), kind=kOutput, calls=%fused_computation.7 | convolution fusion | flops 17188257792 | bytes 46137344 | tf_op jit(solution)/shard_map/rk,nqbk->rqnb/dot_general | solution.py:79
  964.2 31.9 %copy.80 = f32[2048,16,2,128]{3,0,2,1:T(8,128)} copy(f32[2048,16,2,128]{0,3,1,2:T(8,128)} %convolution_bitcast_fusion) | data formatting | bytes 67108864 | tf_op jit(solution)/shard_map/rk,nqbk->rqnb/transpose | solution.py:79
  996.1 41.6 %fusion = f32[16,1,128,32,1,128]{5,3,0,2,4,1:T(8,128)} fusion(f32[16,128,32,128]{3,2,0,1:T(8,128)} %bitcast_add_fusion, f32[16,128,32,128]{3,1,0,2:T(8,128)} %bitcast.155, pred[16,32]{1,0:T(8,128)(4,1)S(1)} %broadcast_and_fusion), kind=kLoop, calls=%fused_computation.5 | loop fusion | flops 16777216 | bytes 100663808 | tf_op jit(solution)/shard_map/reshape | solution.py:92
  1037.7 38.6 %copy.83 = f32[16,1,128,32,1,128]{5,4,3,2,1,0:T(1,128)} copy(f32[16,1,128,32,1,128]{5,3,0,2,4,1:T(8,128)} %fusion) | data formatting | bytes 67108864
  (175 shorter events, 287.4 us)
Async XLA Ops:
  22.1 33.5 %all-to-all-start.1 = ((s32[32,1,8]{2,1,0:T(1,128)}), s32[32,1,8]{2,1,0:T(1,128)S(1)}, u32[]{:S(2)}, u32[]{:S(2)}) async-start(s32[32,1,8]{2,1,0:T(1,128)} %copy.65), calls=%async_computation.1 | async-start | bytes 32768 | tf_op jit(solution)/shard_map/all_to_all | solution.py:38
  55.6 187.0 %all-to-all-start = ((bf16[32,8,128,128]{3,2,1,0:T(8,128)(2,1)}), bf16[32,8,128,128]{3,2,1,0:T(8,128)(2,1)}, u32[]{:S(2)}, u32[]{:S(2)}) async-start(bf16[32,8,128,128]{3,2,1,0:T(8,128)(2,1)} %scatter_fusion), calls=%async_computation | async-start | bytes 16777216 | tf_op jit(solution)/shard_map/all_to_all | solution.py:37
  61.6 281.7 %all-gather.9.cloned.1.call-start = ((), (), s32[]{:S(2)}) async-start(), calls=%async_computation.5 | async-start | bytes 2228224 | tf_op jit(solution)/shard_map/all_gather | solution.py:54
  278.8 106.1 %all-reduce.7.cloned.1.call-start = ((), (), s32[]{:S(2)}) async-start(), calls=%async_computation.6 | async-start | bytes 8388608 | tf_op jit(solution)/shard_map/psum | solution.py:11
  357.5 366.8 %all-gather.5.cloned.1.call-start = ((), (), s32[]{:S(2)}) async-start(), calls=%async_computation.2 | async-start | bytes 10485760 | tf_op jit(solution)/shard_map/all_gather | solution.py:64
  364.3 553.3 %all-reduce.5.cloned.1.call-start = ((), (), s32[]{:S(2)}) async-start(), calls=%async_computation.3 | async-start | bytes 8388608 | tf_op jit(solution)/shard_map/psum | solution.py:11
  384.9 2.2 copy-start.7
  387.3 2.0 copy-start
  412.9 2.0 copy-start.2
  724.3 16.8 %copy-start.11 = (f32[8,128,128]{1,2,0:T(8,128)}, f32[8,128,128]{1,2,0:T(8,128)S(1)}, u32[]{:S(2)}) copy-start(f32[8,128,128]{1,2,0:T(8,128)S(1)} %custom-call.70) | copy-start | bytes 1572868
  759.5 1.0 copy-start.3
  791.9 10.0 copy-start.4
  791.9 10.2 copy-start.5
  791.9 10.4 copy-start.6
  801.9 1.0 copy-start.8
  801.9 1.2 copy-start.9
  801.9 1.4 copy-start.10
  806.8 5.4 copy-start.1
  812.2 126.7 %all-gather.7.cloned.1.call-start = ((), (), s32[]{:S(2)}) async-start(), calls=%async_computation.4 | async-start | bytes 12582912 | tf_op jit(solution)/shard_map/all_gather | solution.py:82
Sparse Core Ops, SparseCore 0:
  278.9 64.3 all-gather.8
  357.6 27.1 all-reduce.6
  812.3 105.2 all-reduce.4
  919.0 19.8 all-gather.6
Sparse Core Ops, SparseCore 1:
  364.3 148.1 all-gather.4
where the time goes:
time: 1090 us; the launch traced here: 1080 us
  waiting for transfers between devices  375 us (34%)
  other arithmetic  322 us (30%)
  local copies, waits for them, and re-layouts  208 us (19%)
  matrix products  144 us (13%)
  between operations  20.9 us (2%)
  starting transfers between devices  14 us (1%)
    all_to_all x1, waiting for transfers between devices, local(): lax.all_to_all(outgoing, ('sub', 'row', 'col'), split_axis=0, concat_axis...  180 us
    another operation x30, other arithmetic, local(): factor = jnp.linalg.cholesky(symmetric)  172 us
    psum x2, waiting for transfers between devices, broadcast(): return lax.psum(block, axis)  126 us
    another operation x3, other arithmetic, local(): jax.scipy.linalg.solve_triangular(factor, widened.T, lower=True)  84.3 us
    all_gather x1, waiting for transfers between devices, local(): beside_all = lax.all_gather(corner, ('row', 'col'), axis=0, tiled=True)  63.9 us
    another operation x15, matrix products, local(): jax.scipy.linalg.solve_triangular(factor, widened.T, lower=True)  61.6 us
    unnamed x35, local copies, waits for them, and re-layouts  49.6 us
    reshape x1, other arithmetic, local(): return (result.reshape(front.shape), panel_out)  41.6 us
  transfers between devices with their start and end apart: 7, of which 5 were waited for; matrix products, arithmetic and copies ran while one was open for 35% of the time, Pallas kernels for 0%

commit v1 on v0

v1 whole, which is shorter than its diff:
```python
import functools

import jax
import jax.numpy as jnp
from jax import lax
from jax.experimental import pallas as pl
from jax.experimental.pallas import tpu as pltpu
from jax.sharding import PartitionSpec as P

NB = 1024
ANY = pl.ANY
EXACT = lax.Precision.HIGHEST
VMEM_LIMIT = 56 * 1024 * 1024


def params():
    return pltpu.CompilerParams(vmem_limit_bytes=VMEM_LIMIT)


def contract(a, b, dim_a, dim_b):
    return lax.dot_general(
        a, b, (((dim_a,), (dim_b,)), ((), ())), precision=EXACT, preferred_element_type=jnp.float32
    )


def pack_kernel(owner, slot, tiles, outgoing, targets, counts, sem, *, capacity):
    tile_count = tiles.shape[0]
    dev_count = counts.shape[0]

    def clear(d, _):
        counts[d] = 0
        for r in range(capacity):
            targets[d * capacity + r] = -1
        return 0

    lax.fori_loop(0, dev_count, clear, 0)

    def send(k, _):
        d = owner[k]
        place = d * capacity + counts[d]
        counts[d] = counts[d] + 1
        targets[place] = slot[k]
        pltpu.make_async_copy(tiles.at[k], outgoing.at[place], sem).start()
        return 0

    lax.fori_loop(0, tile_count, send, 0)
    pltpu.make_async_copy(tiles, outgoing.at[pl.ds(0, tile_count)], sem).wait()


def pack(owner, slot, tiles, dev_count, capacity):
    smem = pl.BlockSpec(memory_space=pltpu.SMEM)
    return pl.pallas_call(
        functools.partial(pack_kernel, capacity=capacity),
        in_specs=[smem, smem, pl.BlockSpec(memory_space=ANY)],
        out_specs=[pl.BlockSpec(memory_space=ANY), smem],
        out_shape=[
            jax.ShapeDtypeStruct((dev_count * capacity,) + tiles.shape[1:], tiles.dtype),
            jax.ShapeDtypeStruct((dev_count * capacity,), jnp.int32),
        ],
        scratch_shapes=[pltpu.SMEM((dev_count,), jnp.int32), pltpu.SemaphoreType.DMA],
        compiler_params=params(),
        cost_estimate=pl.CostEstimate(flops=0, bytes_accessed=2 * tiles.size * 2, transcendentals=0),
        name="pack_children",
    )(owner, slot, tiles)


def eliminate(tile):
    n = tile.shape[0]
    groups = n // 8
    rows = lax.broadcasted_iota(jnp.int32, (8, n), 0)
    lanes = lax.broadcasted_iota(jnp.int32, (8, n), 1)
    upper = [tile[8 * h : 8 * h + 8, :] for h in range(groups)]
    ops = [jnp.where(lanes == rows + 8 * h, 1.0, 0.0).astype(jnp.float32) for h in range(groups)]
    column = [jnp.broadcast_to(upper[h][:, 0:1], (8, n)) for h in range(groups)]
    for j in range(n):
        g, u = divmod(j, 8)
        inverse = 1.0 / column[g][u : u + 1, :]
        row = upper[g][u : u + 1, :] * inverse
        row_ops = ops[g][u : u + 1, :] * inverse
        ahead = [None] * groups
        if j + 1 < n:
            g1, u1 = divmod(j + 1, 8)
            scale = column[g1][u1 : u1 + 1, :] * inverse
            for h in range(g1, groups):
                ahead[h] = jnp.broadcast_to(upper[h][:, j + 1 : j + 2], (8, n)) - column[h] * scale
        for h in range(g, groups):
            below = column[h]
            if h == g:
                below = jnp.where(rows > u, below, 0.0)
            upper[h] = upper[h] - below * row
            ops[h] = ops[h] - below * row_ops
        column = ahead
    return jnp.concatenate(upper, 0), jnp.concatenate(ops, 0)


def factor_kernel(corner, lower, inverse, work, copied, sem, *, tiles, per_col, col_count):
    t = corner.shape[-1]
    rows = lax.broadcasted_iota(jnp.int32, (t, t), 0)
    cols = lax.broadcasted_iota(jnp.int32, (t, t), 1)
    copies = []
    for p in range(tiles):
        for j in range(p + 1):
            copies.append(
                pltpu.make_async_copy(
                    corner.at[p * col_count + j % col_count, j // col_count], copied.at[p, j], sem
                )
            )
    for copy in copies:
        copy.start()
    lower[...] = jnp.zeros_like(lower)
    for copy in copies:
        copy.wait()

    for p in range(tiles):
        for j in range(p + 1):
            block = copied[p, j]
            if p == j:
                block = jnp.where(rows >= cols, block, block.T)
                work[p, :, p * t : (p + 1) * t] = block
            else:
                work[p, :, j * t : (j + 1) * t] = block
                work[j, :, p * t : (p + 1) * t] = block.T

    def step(j, _):
        here = pl.ds(pl.multiple_of(j * t, t), t)
        upper, ops = eliminate(work[j, :, here])
        pivots = jnp.sum(jnp.where(rows == cols, upper, 0.0), 1, keepdims=True)
        scale = lax.rsqrt(pivots)
        upper = jnp.where(rows <= cols, upper * scale, 0.0)
        ops = jnp.where(rows >= cols, ops * scale, 0.0)
        lower[pl.ds(pl.multiple_of(j * t, t), t), here] = upper.T.astype(lower.dtype)
        work[j, :, here] = jnp.where(rows == cols, 1.0, 0.0)
        work[j] = contract(ops, work[j], 1, 0)

        def below(i, _):
            block = contract(work[i, :, here], ops, 1, 1)
            lower[pl.ds(pl.multiple_of(i * t, t), t), here] = block.astype(lower.dtype)
            work[i, :, here] = jnp.zeros((t, t), jnp.float32)
            work[i] = work[i] - contract(block, work[j], 1, 0)
            return 0

        lax.fori_loop(j + 1, tiles, below, 0)
        return 0

    lax.fori_loop(0, tiles, step, 0)
    wide_rows = lax.broadcasted_iota(jnp.int32, (t, tiles * t), 1)
    for p in range(tiles):
        inverse[p * t : (p + 1) * t, :] = jnp.where(wide_rows < (p + 1) * t, work[p], 0.0)


def factor(corner, tiles, per_col, col_count):
    t = corner.shape[-1]
    n = tiles * t
    vmem = pl.BlockSpec(memory_space=pltpu.VMEM)
    return pl.pallas_call(
        functools.partial(factor_kernel, tiles=tiles, per_col=per_col, col_count=col_count),
        in_specs=[pl.BlockSpec(memory_space=ANY)],
        out_specs=[vmem, vmem],
        out_shape=[jax.ShapeDtypeStruct((n, n), jnp.bfloat16), jax.ShapeDtypeStruct((n, n), jnp.float32)],
        scratch_shapes=[
            pltpu.VMEM((tiles, t, n), jnp.float32),
            pltpu.VMEM((tiles, tiles, t, t), jnp.float32),
            pltpu.SemaphoreType.DMA,
        ],
        compiler_params=params(),
        cost_estimate=pl.CostEstimate(flops=100_000_000_000, bytes_accessed=200_000_000, transcendentals=0),
        name="factor_corner",
    )(corner)


def panel_kernel(landing, front, arrived, out, buf, tiles, picked, in_sem, tile_sem, out_sem, *, per_col, col_tiles):
    slots = landing.shape[0]

    def front_copy(s):
        return pltpu.make_async_copy(front.at[:, :, s, :], buf.at[:, s], in_sem)

    for s in range(per_col):
        front_copy(s).start()

    def find(k, n):
        slot = landing[k]
        hit = jnp.logical_and(slot >= 0, lax.rem(slot, col_tiles) < per_col)

        @pl.when(hit)
        def _():
            picked[n] = slot
            pltpu.make_async_copy(arrived.at[k], tiles.at[n], tile_sem).start()

        return n + hit.astype(jnp.int32)

    found = lax.fori_loop(0, slots, find, 0)
    for s in range(per_col):
        front_copy(s).wait()

    def wait(n, _):
        pltpu.make_async_copy(arrived.at[0], tiles.at[0], tile_sem).wait()
        return 0

    lax.fori_loop(0, found, wait, 0)

    def add(n, _):
        q = picked[n] // col_tiles
        s = lax.rem(picked[n], col_tiles)
        buf[q, s] = buf[q, s] + tiles[n].astype(jnp.float32)
        return 0

    lax.fori_loop(0, found, add, 0)
    copy = pltpu.make_async_copy(buf, out, out_sem)
    copy.start()
    copy.wait()


def assemble_panel(landing, front, arrived, per_col):
    row_tiles, t, col_tiles, _ = front.shape
    any_spec = pl.BlockSpec(memory_space=ANY)
    return pl.pallas_call(
        functools.partial(panel_kernel, per_col=per_col, col_tiles=col_tiles),
        in_specs=[pl.BlockSpec(memory_space=pltpu.SMEM), any_spec, any_spec],
        out_specs=any_spec,
        out_shape=jax.ShapeDtypeStruct((row_tiles, per_col, t, t), jnp.float32),
        scratch_shapes=[
            pltpu.VMEM((row_tiles, per_col, t, t), jnp.float32),
            pltpu.VMEM(arrived.shape, arrived.dtype),
            pltpu.SMEM(landing.shape, jnp.int32),
            pltpu.SemaphoreType.DMA,
            pltpu.SemaphoreType.DMA,
            pltpu.SemaphoreType.DMA,
        ],
        compiler_params=params(),
        cost_estimate=pl.CostEstimate(flops=0, bytes_accessed=20_000_000, transcendentals=0),
        name="assemble_panel",
    )(landing, front, arrived)


def update_kernel(
    landing, front, panel, left, right, arrived, out,
    buf, left_v, right_v, tiles, head, following,
    in_sem, out_sem, left_sem, right_sem, tile_sem, panel_sem,
    *, per_col, sub_count, span, depth, together,
):
    row_tiles, t, col_tiles, _ = front.shape
    slots = landing.shape[0]
    steps = row_tiles // span
    wide = col_tiles - per_col

    def read(i, slot, s):
        return pltpu.make_async_copy(
            front.at[pl.ds(i * span, span), :, per_col + s, :], buf.at[slot, s], in_sem.at[slot]
        )

    def write(i, slot, s):
        return pltpu.make_async_copy(
            buf.at[slot, s], out.at[pl.ds(i * span, span), :, per_col + s, :], out_sem.at[slot]
        )

    def read_all(i, slot):
        for s in range(wide):
            read(i, slot, s).start()

    def right_copy(s):
        c = per_col + s
        return pltpu.make_async_copy(
            right.at[c % sub_count, c // sub_count], right_v.at[s], right_sem.at[s // together]
        )

    left_copy = pltpu.make_async_copy(left, left_v, left_sem)
    left_copy.start()
    for s in range(wide):
        right_copy(s).start()
    read_all(0, 0)
    tile_copy = pltpu.make_async_copy(arrived, tiles, tile_sem)
    tile_copy.start()
    panel_copies = [
        pltpu.make_async_copy(panel.at[:, s], out.at[:, :, s, :], panel_sem.at[s]) for s in range(per_col)
    ]

    def clear(q, _):
        head[q] = -1
        return 0

    lax.fori_loop(0, row_tiles, clear, 0)

    def link(k, _):
        slot = landing[k]

        @pl.when(jnp.logical_and(slot >= 0, lax.rem(slot, col_tiles) >= per_col))
        def _():
            q = slot // col_tiles
            following[k] = head[q]
            head[q] = k

        return 0

    lax.fori_loop(0, slots, link, 0)
    left_copy.wait()

    def step(i, _):
        slot = lax.rem(i, depth)

        @pl.when(i + 1 < steps)
        def _():
            later = lax.rem(i + 1, depth)

            @pl.when(i + 1 >= depth)
            def _():
                for s in range(wide):
                    write(0, later, s).wait()

            read_all(i + 1, later)

        rows = left_v[pl.ds(i * span, span)].reshape(span * t, left_v.shape[-1])
        for s in range(wide):
            read(0, slot, s).wait()
        for s in range(0, wide, together):
            @pl.when(i == 0)
            def _():
                for o in range(together):
                    right_copy(s + o).wait()

            cols = right_v[s : s + together].reshape(together * t, right_v.shape[-1])
            product = lax.dot_general(
                rows, cols, (((1,), (1,)), ((), ())), preferred_element_type=jnp.float32
            )
            for o in range(together):
                piece = product[:, o * t : (o + 1) * t].reshape(span, t, t)
                buf[slot, s + o] = buf[slot, s + o] - piece

        @pl.when(i == 0)
        def _():
            tile_copy.wait()
            for copy in panel_copies:
                copy.start()

        for d in range(span):

            def add(k):
                s = lax.rem(landing[k], col_tiles) - per_col
                buf[slot, s, d] = buf[slot, s, d] + tiles[k].astype(jnp.float32)
                return following[k]

            lax.while_loop(lambda k: k >= 0, add, head[i * span + d])

        for s in range(wide):
            write(i, slot, s).start()
        return 0

    lax.fori_loop(0, steps, step, 0)
    for i in range(max(0, steps - depth), steps):
        for s in range(wide):
            write(0, i % depth, s).wait()
    for copy in panel_copies:
        copy.wait()


def update(landing, front, panel, left, right, arrived, per_col):
    row_tiles, t, col_tiles, _ = front.shape
    sub_count = right.shape[0]
    span = 2 if row_tiles % 2 == 0 else 1
    depth = 3
    wide = col_tiles - per_col
    together = 2 if wide % 2 == 0 else 1
    any_spec = pl.BlockSpec(memory_space=ANY)
    return pl.pallas_call(
        functools.partial(
            update_kernel, per_col=per_col, sub_count=sub_count, span=span, depth=depth, together=together
        ),
        in_specs=[pl.BlockSpec(memory_space=pltpu.SMEM)] + [any_spec] * 5,
        out_specs=any_spec,
        out_shape=jax.ShapeDtypeStruct(front.shape, jnp.float32),
        scratch_shapes=[
            pltpu.VMEM((depth, wide, span, t, t), jnp.float32),
            pltpu.VMEM(left.shape, left.dtype),
            pltpu.VMEM((wide, t, left.shape[-1]), right.dtype),
            pltpu.VMEM(arrived.shape, arrived.dtype),
            pltpu.SMEM((row_tiles,), jnp.int32),
            pltpu.SMEM(landing.shape, jnp.int32),
            pltpu.SemaphoreType.DMA((depth,)),
            pltpu.SemaphoreType.DMA((depth,)),
            pltpu.SemaphoreType.DMA,
            pltpu.SemaphoreType.DMA((wide // together,)),
            pltpu.SemaphoreType.DMA,
            pltpu.SemaphoreType.DMA((per_col,)),
        ],
        compiler_params=params(),
        cost_estimate=pl.CostEstimate(
            flops=2 * row_tiles * t * wide * t * left.shape[-1],
            bytes_accessed=2 * front.size * 4,
            transcendentals=0,
        ),
        name="trailing_update",
    )(landing, front, panel, left, right, arrived)


def across_rows(mine, row_index, col_index, row_count, col_count):
    if row_count != 4 or col_count != 4:
        return lax.psum(jnp.where(row_index == col_index, mine, jnp.zeros_like(mine)), "row")
    role = row_index ^ col_index
    half = mine.shape[0] // 2
    first, second = mine[:half], mine[half:]

    def hop(value, moves):
        pairs = []
        for c in range(col_count):
            for a, b in moves:
                pairs.append(((c ^ a) * col_count + c, (c ^ b) * col_count + c))
        return lax.ppermute(value, ("row", "col"), pairs)

    first_1 = hop(first, [(0, 1)])
    second_1 = hop(second, [(0, 2)])
    first_2 = hop(jnp.where(role == 0, first, first_1), [(0, 2), (1, 3)])
    second_2 = hop(jnp.where(role == 0, second, second_1), [(0, 1), (2, 3)])
    first = jnp.where(role == 0, first, jnp.where(role == 1, first_1, first_2))
    second = jnp.where(role == 0, second, jnp.where(role == 2, second_1, second_2))
    return jnp.concatenate([first, second], 0)


def local(front, child_tiles, tile_owner, tile_slot):
    row_tiles, _, t, col_tiles, _, _ = front.shape
    sub_count = lax.axis_size("sub")
    row_count = lax.axis_size("row")
    col_count = lax.axis_size("col")
    dev_count = sub_count * row_count * col_count
    tile_count = child_tiles.shape[0]
    capacity = max(2, 2 * tile_count // dev_count)
    panel_tiles = NB // t
    per_col = panel_tiles // col_count
    part = row_tiles // col_count
    local_front = front.reshape(row_tiles, t, col_tiles, t)
    sub_index = lax.axis_index("sub")
    row_index = lax.axis_index("row")
    col_index = lax.axis_index("col")
    group_id = sub_index * row_count + row_index

    corner = local_front[0, :, :per_col, :].transpose(1, 0, 2)
    corner = lax.all_gather(corner, ("sub", "row", "col"), axis=0)

    outgoing, targets = pack(tile_owner[:, 0], tile_slot, child_tiles, dev_count, capacity)
    landing = lax.all_to_all(
        targets.reshape(dev_count, capacity), ("sub", "row", "col"), split_axis=0, concat_axis=0, tiled=True
    ).reshape(dev_count * capacity)
    arrived = lax.all_to_all(
        outgoing.reshape(dev_count, capacity, t, t), ("sub", "row", "col"), split_axis=0, concat_axis=0, tiled=True
    ).reshape(dev_count * capacity, t, t)
    lower, inverse = factor(corner, panel_tiles, per_col, col_count)

    panel = assemble_panel(landing, local_front, arrived, per_col)
    shared = lax.all_to_all(
        panel.reshape(col_count, part, per_col, t, t), "col", split_axis=0, concat_axis=0, tiled=True
    )
    shared = shared.transpose(1, 3, 2, 0, 4).reshape(part * t, NB)
    solved = contract(shared, inverse, 1, 1).astype(jnp.bfloat16).reshape(part, t, NB)
    leading = lax.dynamic_slice_in_dim(lower, jnp.minimum(group_id, panel_tiles - 1) * t, t, 0)
    is_leading = group_id < panel_tiles
    upper = jnp.where(jnp.logical_and(is_leading, col_index == 0), leading, solved[0])
    solved = jnp.concatenate([upper[None], solved[1:]], 0)
    rows = lax.all_gather(solved, "col", axis=0, tiled=True)
    panel_out = lax.dynamic_index_in_dim(
        rows.reshape(row_tiles, t, per_col, col_count, t), col_index, 3, keepdims=True
    ).reshape(row_tiles, 1, t, per_col, 1, t)
    across = across_rows(rows, row_index, col_index, row_count, col_count)
    right = lax.all_gather(across, "sub", axis=0)
    left = jnp.concatenate([jnp.where(is_leading, jnp.zeros_like(rows[:1]), rows[:1]), rows[1:]], 0)
    result = update(landing, local_front, panel, left, right, arrived, per_col)
    return (result.reshape(front.shape), panel_out)


def solution(mesh):
    return jax.shard_map(
        local,
        mesh=mesh,
        in_specs=(
            P(None, ("sub", "row"), None, None, "col", None),
            P(("sub", "row", "col"), None, None),
            P(("sub", "row", "col"), None),
            P(("sub", "row", "col")),
        ),
        out_specs=(
            P(None, ("sub", "row"), None, None, "col", None),
            P(None, ("sub", "row"), None, None, "col", None),
        ),
        check_vma=False,
    )
```

time: 1090 us -> 857 us (0.79)
  other arithmetic: 322 us -> 19.2 us
  Pallas kernels: 0 us -> 289 us
  local copies, waits for them, and re-layouts: 208 us -> 30.8 us
  matrix products: 144 us -> 8.68 us
  waiting for transfers between devices: 375 us -> 455 us
  blocking collectives: 0 us -> 14.2 us
  starting transfers between devices: 14 us -> 25.4 us
    pallas_call x0 -> x4, Pallas kernels: none -> 289 us  [the longest x1 130 us: pack(): pl.pallas_call(functools.partial(pack_kernel, capacity=capacity), in_spec...]
    another operation x34 -> x0, other arithmetic: 256 us -> none  [the longest x30 172 us: local(): factor = jnp.linalg.cholesky(symmetric)]
    ppermute x0 -> x4, waiting for transfers between devices: none -> 173 us  [hop(): return lax.ppermute(value, ('row', 'col'), pairs)]
    psum x2 -> x0, waiting for transfers between devices: 126 us -> none  [broadcast(): return lax.psum(block, axis)]
    another operation x29 -> x0, matrix products: 84.7 us -> none  [the longest x15 61.6 us: local(): jax.scipy.linalg.solve_triangular(factor, widened.T, lower=True)]
    dot_general x2 -> x1, matrix products: 59.8 us -> 8.68 us  [contract(): lax.dot_general(a, b, (((dim_a,), (dim_b,)), ((), ())), precision=EXACT,...]
    unnamed x35 -> x7, local copies, waits for them, and re-layouts: 49.6 us -> 4.93 us
    reshape x1 -> x0, other arithmetic: 41.6 us -> none  [local(): return (result.reshape(front.shape), panel_out)]
  transfers between devices with their start and end apart: 7 -> 9, of which waited for: 5 -> 7; matrix products, arithmetic and copies ran while one was open for 35% -> 2% of each run, Pallas kernels for 0% -> 9%
where the time goes in v1:
time: 857 us; the launch traced here: 856 us
  waiting for transfers between devices  455 us (53%)
  Pallas kernels  289 us (34%)
  local copies, waits for them, and re-layouts  30.8 us (4%)
  starting transfers between devices  25.4 us (3%)
  other arithmetic  19.2 us (2%)
  blocking collectives  14.2 us (2%)
  between operations  13.9 us (2%)
  matrix products  8.68 us (1%)
    all_to_all x1, waiting for transfers between devices, local(): lax.all_to_all(outgoing.reshape(dev_count, capacity, t, t), ('sub', 'row'...  197 us
    ppermute x4, waiting for transfers between devices, hop(): return lax.ppermute(value, ('row', 'col'), pairs)  173 us
    pallas_call x1, Pallas kernels, pack(): pl.pallas_call(functools.partial(pack_kernel, capacity=capacity), in_spec...  130 us
    all_gather x1, waiting for transfers between devices, local(): rows = lax.all_gather(solved, 'col', axis=0, tiled=True)  80.7 us
    pallas_call x1, Pallas kernels, update(): pl.pallas_call(functools.partial(update_kernel, per_col=per_col, sub_coun...  78.4 us
    pallas_call x1, Pallas kernels, factor(): pl.pallas_call(functools.partial(factor_kernel, tiles=tiles, per_col=per_...  75.5 us
  transfers between devices with their start and end apart: 9, of which 7 were waited for; matrix products, arithmetic and copies ran while one was open for 2% of the time, Pallas kernels for 9%

profile of v1, /device:TPU:0, one launch (start us, length us, event | category | flops | bytes accessed | tf_op | source)
XLA Modules:
  0.0 855.9 jit_solution(9866508739419658113)
XLA Ops:
  7.2 129.8 %pack_children.1 = (bf16[256,128,128]{2,1,0:T(8,128)(2,1)}, s32[256]{0:T(256)}) custom-call(s32[128]{0:T(128)} %bitcast.35, s32[128]{0:T(128)} %slot.1, bf16[128,128,128]{2,1,0:T(8,128)(2,1)} %tiles.1), custom_call_target="tpu_custom_call" | custom-call | bytes 8388608 | tf_op jit(solution)/shard_map/pack_children/pallas_call | solution.py:52
  137.7 14.2 %all_to_all.19 = s32[32,1,8]{2,1,0:T(1,128)S(1)} all-to-all(s32[32,1,8]{2,1,0:T(1,128)S(1)} %bitcast.34), channel_id=1, replica_groups=mesh['sub'=2,'row'=4,'col'=4] {'sub','row','col'}, dimensions={0} | all-to-all | bytes 2048 | tf_op jit(solution)/shard_map/all_to_all | solution.py:438
  151.9 3.7 all-to-all-start.1
  159.3 197.1 %all-to-all-done.1 = bf16[32,8,128,128]{3,2,1,0:T(8,128)(2,1)} async-done(((bf16[32,8,128,128]{3,2,1,0:T(8,128)(2,1)}), bf16[32,8,128,128]{3,2,1,0:T(8,128)(2,1)}, u32[]{:S(2)}, u32[]{:S(2)}) %all-to-all-start.1) | async-done | bytes 8388640 | tf_op jit(solution)/shard_map/all_to_all | solution.py:441
  356.4 5.4 assemble_panel.1.panel
  361.8 4.5 copy.21
  366.3 8.3 all-to-all-start.2
  374.6 75.5 %factor_corner.1 = (bf16[1024,1024]{1,0:T(8,128)(2,1)}, f32[1024,1024]{1,0:T(8,128)}) custom-call(f32[32,2,128,128]{3,2,1,0:T(8,128)} %bitcast.36), custom_call_target="tpu_custom_call" | custom-call | flops 99999997952 | bytes 200000000 | tf_op jit(solution)/shard_map/factor_corner/pallas_call | solution.py:155
  450.2 2.7 copy.22
  455.0 8.7 %convolution_convert_fusion = bf16[512,1024]{1,0:T(8,128)(2,1)S(1)} fusion(f32[512,1024]{1,0:T(8,128)S(1)} %reshape.45, f32[1024,1024]{1,0:T(8,128)} %get-tuple-element.9), kind=kOutput, calls=%fused_computation.6 | convolution fusion | flops 6442975232 | bytes 7340032 | tf_op jit(solution)/shard_map/dot_general | solution.py:21
  465.9 80.7 %all-gather.6.cloned.1.call-done = bf16[16,128,1024]{2,1,0:T(8,128)(2,1)} async-done(((bf16[4,128,1024]{2,1,0:T(8,128)(2,1)}), bf16[16,128,1024]{2,1,0:T(8,128)(2,1)}) %all-gather.6.cloned.1.call-update) | async-done | bytes 4194320 | tf_op jit(solution)/shard_map/all_gather | solution.py:456
  546.6 3.1 slice.38
  549.7 3.5 collective-permute-start
  553.2 45.0 %collective-permute-done = bf16[8,128,1024]{2,1,0:T(8,128)(2,1)S(1)} collective-permute-done((bf16[8,128,1024]{2,1,0:T(8,128)(2,1)}, bf16[8,128,1024]{2,1,0:T(8,128)(2,1)S(1)}, u32[]{:S(2)}, u32[]{:S(2)}) %collective-permute-start) | collective-permute-done | bytes 2097184 | tf_op jit(solution)/shard_map/ppermute | solution.py:406
  598.2 3.1 broadcast_select_fusion.1
  604.0 43.2 %collective-permute-done.1 = bf16[8,128,1024]{2,1,0:T(8,128)(2,1)} collective-permute-done((bf16[8,128,1024]{2,1,0:T(8,128)(2,1)}, bf16[8,128,1024]{2,1,0:T(8,128)(2,1)}, u32[]{:S(2)}, u32[]{:S(2)}) %collective-permute-start.1) | collective-permute-done | bytes 2097184 | tf_op jit(solution)/shard_map/ppermute | solution.py:406
  647.2 4.6 select_select_fusion.1
  651.8 4.5 collective-permute-start.2
  656.3 43.2 %collective-permute-done.2 = bf16[8,128,1024]{2,1,0:T(8,128)(2,1)S(1)} collective-permute-done((bf16[8,128,1024]{2,1,0:T(8,128)(2,1)S(1)}, bf16[8,128,1024]{2,1,0:T(8,128)(2,1)S(1)}, u32[]{:S(2)}, u32[]{:S(2)}) %collective-permute-start.2) | collective-permute-done | bytes 2097184 | tf_op jit(solution)/shard_map/ppermute | solution.py:406
  703.7 41.6 %collective-permute-done.3 = bf16[8,128,1024]{2,1,0:T(8,128)(2,1)} collective-permute-done((bf16[8,128,1024]{2,1,0:T(8,128)(2,1)}, bf16[8,128,1024]{2,1,0:T(8,128)(2,1)}, u32[]{:S(2)}, u32[]{:S(2)}) %collective-permute-start.3) | collective-permute-done | bytes 2097184 | tf_op jit(solution)/shard_map/ppermute | solution.py:406
  750.3 6.5 copy.23
  760.2 2.9 copy-done.1
  767.2 3.7 all-gather.10.cloned.1.call-done
  771.0 78.4 %trailing_update.1 = f32[16,128,32,128]{3,2,1,0:T(8,128)} custom-call(s32[256]{0:T(256)} %reshape.40.landing, f32[16,128,32,128]{3,2,1,0:T(8,128)} %bitcast.26, f32[16,2,128,128]{3,2,1,0:T(8,128)} %assemble_panel.1.panel, bf16[16,128,1024]{2,1,0:T(8,128)(2,1)} %pad_maximum_fusion.left, bf16[2,16,128,1024]{3,2,1,0:T(8,128)(2,1)} %bitcast.29, ...), custom_call_target="tpu_custom_call" | custom-call | flops 16106127360 | bytes 67108864 | tf_op jit(solution)/shard_map/trailing_update/pallas_call | solution.py:363
  (34 shorter events, 28.0 us)
Async XLA Ops:
  151.9 204.5 %all-to-all-start.1 = ((bf16[32,8,128,128]{3,2,1,0:T(8,128)(2,1)}), bf16[32,8,128,128]{3,2,1,0:T(8,128)(2,1)}, u32[]{:S(2)}, u32[]{:S(2)}) async-start(bf16[32,8,128,128]{3,2,1,0:T(8,128)(2,1)} %bitcast.30), calls=%async_computation.1 | async-start | bytes 16777216 | tf_op jit(solution)/shard_map/all_to_all | solution.py:441
  155.6 219.0 %all-gather.8.cloned.1.call-start = ((), (), s32[]{:S(2)}) async-start(), calls=%async_computation.4 | async-start | bytes 4325376 | tf_op jit(solution)/shard_map/all_gather | solution.py:435
  366.3 83.9 %all-to-all-start.2 = ((f32[4,4,2,128,128]{4,2,3,1,0:T(2,128)}), f32[4,4,2,128,128]{4,2,3,1,0:T(2,128)S(1)}, u32[]{:S(2)}, u32[]{:S(2)}) async-start(f32[4,4,2,128,128]{4,2,3,1,0:T(2,128)} %copy.21), calls=%async_computation.2 | async-start | bytes 4194304 | tf_op jit(solution)/shard_map/all_to_all | solution.py:447
  374.6 172.0 %all-gather.6.cloned.1.call-start = ((), (), s32[]{:S(2)}) async-start(), calls=%async_computation.3 | async-start | bytes 5242880 | tf_op jit(solution)/shard_map/all_gather | solution.py:456
  465.9 305.1 %all-gather.10.cloned.1.call-start = ((), (), s32[]{:S(2)}) async-start(), calls=%async_computation.5 | async-start | bytes 12582912 | tf_op jit(solution)/shard_map/all_gather | solution.py:461
  549.7 48.6 %collective-permute-start = (bf16[8,128,1024]{2,1,0:T(8,128)(2,1)}, bf16[8,128,1024]{2,1,0:T(8,128)(2,1)S(1)}, u32[]{:S(2)}, u32[]{:S(2)}) collective-permute-start(bf16[8,128,1024]{2,1,0:T(8,128)(2,1)} %slice.38), channel_id=1, source_target_pairs={{0,4},{5,1},{10,14},{15,11},{16,20},{21,17},{26,30},{31,27}} | collective-permute-start | bytes 6291464 | tf_op jit(solution)/shard_map/ppermute | solution.py:406
  601.4 45.8 %collective-permute-start.1 = (bf16[8,128,1024]{2,1,0:T(8,128)(2,1)}, bf16[8,128,1024]{2,1,0:T(8,128)(2,1)}, u32[]{:S(2)}, u32[]{:S(2)}) collective-permute-start(bf16[8,128,1024]{2,1,0:T(8,128)(2,1)} %broadcast_select_fusion.1), channel_id=1, source_target_pairs={{0,8},{4,12},{5,13},{1,9},{10,2},{14,6},{15,7},{11,3},{16,24},{20,... | collective-permute-start | bytes 6291464 | tf_op jit(solution)/shard_map/ppermute | solution.py:406
  604.0 95.5 %copy-start = (bf16[16,128,1024]{2,1,0:T(8,128)(2,1)S(1)}, bf16[16,128,1024]{2,1,0:T(8,128)(2,1)}, u32[]{:S(2)}) copy-start(bf16[16,128,1024]{2,1,0:T(8,128)(2,1)} %all-gather.6.cloned.1.call-done) | copy-start | bytes 12582916
  651.8 47.7 %collective-permute-start.2 = (bf16[8,128,1024]{2,1,0:T(8,128)(2,1)S(1)}, bf16[8,128,1024]{2,1,0:T(8,128)(2,1)S(1)}, u32[]{:S(2)}, u32[]{:S(2)}) collective-permute-start(bf16[8,128,1024]{2,1,0:T(8,128)(2,1)S(1)} %get-tuple-element.19), channel_id=1, source_target_pairs={{0,8},{5,13},{10,2},{15,7},{16,24},{21,29},{26,18},{31,23}} | collective-permute-start | bytes 6291464 | tf_op jit(solution)/shard_map/ppermute | solution.py:406
  701.1 44.3 %collective-permute-start.3 = (bf16[8,128,1024]{2,1,0:T(8,128)(2,1)}, bf16[8,128,1024]{2,1,0:T(8,128)(2,1)}, u32[]{:S(2)}, u32[]{:S(2)}) collective-permute-start(bf16[8,128,1024]{2,1,0:T(8,128)(2,1)} %broadcast_select_fusion), channel_id=1, source_target_pairs={{0,4},{8,12},{5,1},{13,9},{10,14},{2,6},{15,11},{7,3},{16,20},{24,... | collective-permute-start | bytes 6291464 | tf_op jit(solution)/shard_map/ppermute | solution.py:406
  703.7 44.2 %copy-start.2 = (bf16[8,128,1024]{2,1,0:T(8,128)(2,1)S(1)}, bf16[8,128,1024]{2,1,0:T(8,128)(2,1)}, u32[]{:S(2)}) copy-start(bf16[8,128,1024]{2,1,0:T(8,128)(2,1)} %get-tuple-element.18) | copy-start | bytes 6291460
  760.2 2.9 copy-start.1
  760.2 4.7 slice-start
Sparse Core Ops, SparseCore 0:
  160.0 124.7 all-gather.7
  466.0 80.5 all-gather.5
  750.4 20.5 all-gather.9

commit v2 on v1

--- a/solution.py
+++ b/solution.py
@@ -23,9 +23,11 @@
     )
 
 
-def pack_kernel(owner, slot, tiles, outgoing, targets, counts, sem, *, capacity):
+def pack_kernel(owner, slot, tiles, outgoing, targets, counts, held, in_sem, sem, *, capacity):
     tile_count = tiles.shape[0]
     dev_count = counts.shape[0]
+    load = pltpu.make_async_copy(tiles, held, in_sem)
+    load.start()
 
     def clear(d, _):
         counts[d] = 0
@@ -34,17 +36,18 @@
         return 0
 
     lax.fori_loop(0, dev_count, clear, 0)
+    load.wait()
 
     def send(k, _):
         d = owner[k]
         place = d * capacity + counts[d]
         counts[d] = counts[d] + 1
         targets[place] = slot[k]
-        pltpu.make_async_copy(tiles.at[k], outgoing.at[place], sem).start()
+        pltpu.make_async_copy(held.at[k], outgoing.at[place], sem).start()
         return 0
 
     lax.fori_loop(0, tile_count, send, 0)
-    pltpu.make_async_copy(tiles, outgoing.at[pl.ds(0, tile_count)], sem).wait()
+    pltpu.make_async_copy(held, outgoing.at[pl.ds(0, tile_count)], sem).wait()
 
 
 def pack(owner, slot, tiles, dev_count, capacity):
@@ -57,7 +60,12 @@
             jax.ShapeDtypeStruct((dev_count * capacity,) + tiles.shape[1:], tiles.dtype),
             jax.ShapeDtypeStruct((dev_count * capacity,), jnp.int32),
         ],
-        scratch_shapes=[pltpu.SMEM((dev_count,), jnp.int32), pltpu.SemaphoreType.DMA],
+        scratch_shapes=[
+            pltpu.SMEM((dev_count,), jnp.int32),
+            pltpu.VMEM(tiles.shape, tiles.dtype),
+            pltpu.SemaphoreType.DMA,
+            pltpu.SemaphoreType.DMA,
+        ],
         compiler_params=params(),
         cost_estimate=pl.CostEstimate(flops=0, bytes_accessed=2 * tiles.size * 2, transcendentals=0),
         name="pack_children",
@@ -233,46 +241,56 @@
 
 
 def update_kernel(
-    landing, front, panel, left, right, arrived, out,
-    buf, left_v, right_v, tiles, head, following,
-    in_sem, out_sem, left_sem, right_sem, tile_sem, panel_sem,
-    *, per_col, sub_count, span, depth, together,
+    landing, place, front, panel, arrived, *rest,
+    per_col, sub_count, span, depth, together, lines, rounds,
 ):
+    left, rest = rest[:lines], rest[lines:]
+    right, rest = rest[:rounds * sub_count], rest[rounds * sub_count :]
+    out, buf, left_v, right_v, tiles, head, following = rest[:7]
+    in_sem, out_sem, left_sem, right_sem, tile_sem = rest[7:]
     row_tiles, t, col_tiles, _ = front.shape
     slots = landing.shape[0]
     steps = row_tiles // span
     wide = col_tiles - per_col
 
     def read(i, slot, s):
-        return pltpu.make_async_copy(
-            front.at[pl.ds(i * span, span), :, per_col + s, :], buf.at[slot, s], in_sem.at[slot]
-        )
+        here = pl.ds(i * span, span)
+        source = panel.at[here, s] if s < per_col else front.at[here, :, s, :]
+        return pltpu.make_async_copy(source, buf.at[slot, s], in_sem.at[slot])
 
     def write(i, slot, s):
         return pltpu.make_async_copy(
-            buf.at[slot, s], out.at[pl.ds(i * span, span), :, per_col + s, :], out_sem.at[slot]
+            buf.at[slot, s], out.at[pl.ds(i * span, span), :, s, :], out_sem.at[slot]
         )
 
     def read_all(i, slot):
-        for s in range(wide):
+        for s in range(col_tiles):
             read(i, slot, s).start()
 
-    def right_copy(s):
-        c = per_col + s
-        return pltpu.make_async_copy(
-            right.at[c % sub_count, c // sub_count], right_v.at[s], right_sem.at[s // together]
-        )
-
-    left_copy = pltpu.make_async_copy(left, left_v, left_sem)
-    left_copy.start()
-    for s in range(wide):
-        right_copy(s).start()
+    part = left[0].shape[0]
+    count = row_tiles // part
+    for k in range(count):
+        for c in range(count):
+
+            @pl.when(place[0] == c)
+            def _(k=k, c=c):
+                piece = left[c - k] if k <= c else left[count - 1 + k - c]
+                pltpu.make_async_copy(piece, left_v.at[pl.ds(k * part, part)], left_sem).start()
+
+    for n in range(rounds):
+        for i in range(sub_count):
+            origin = lax.rem(place[1] + sub_count - i, sub_count)
+            for r in range(part):
+                column = (place[3 + n] * part + r) * sub_count + origin
+
+                @pl.when(column >= per_col)
+                def _(n=n, i=i, r=r, column=column):
+                    pltpu.make_async_copy(
+                        right[n * sub_count + i].at[r], right_v.at[column - per_col], right_sem
+                    ).start()
+
     read_all(0, 0)
     tile_copy = pltpu.make_async_copy(arrived, tiles, tile_sem)
-    tile_copy.start()
-    panel_copies = [
-        pltpu.make_async_copy(panel.at[:, s], out.at[:, :, s, :], panel_sem.at[s]) for s in range(per_col)
-    ]
 
     def clear(q, _):
         head[q] = -1
@@ -292,7 +310,13 @@
         return 0
 
     lax.fori_loop(0, slots, link, 0)
-    left_copy.wait()
+    pltpu.make_async_copy(left_v, left_v, left_sem).wait()
+
+    @pl.when(place[2] == 1)
+    def _():
+        left_v[0] = jnp.zeros_like(left_v[0])
+
+    pltpu.make_async_copy(right_v, right_v, right_sem).wait()
 
     def step(i, _):
         slot = lax.rem(i, depth)
@@ -303,100 +327,112 @@
 
             @pl.when(i + 1 >= depth)
             def _():
-                for s in range(wide):
+                for s in range(col_tiles):
                     write(0, later, s).wait()
 
             read_all(i + 1, later)
 
+        @pl.when(i == 0)
+        def _():
+            tile_copy.start()
+
         rows = left_v[pl.ds(i * span, span)].reshape(span * t, left_v.shape[-1])
-        for s in range(wide):
+        for s in range(col_tiles):
             read(0, slot, s).wait()
         for s in range(0, wide, together):
-            @pl.when(i == 0)
-            def _():
-                for o in range(together):
-                    right_copy(s + o).wait()
-
             cols = right_v[s : s + together].reshape(together * t, right_v.shape[-1])
             product = lax.dot_general(
                 rows, cols, (((1,), (1,)), ((), ())), preferred_element_type=jnp.float32
             )
             for o in range(together):
                 piece = product[:, o * t : (o + 1) * t].reshape(span, t, t)
-                buf[slot, s + o] = buf[slot, s + o] - piece
+                buf[slot, per_col + s + o] = buf[slot, per_col + s + o] - piece
 
         @pl.when(i == 0)
         def _():
             tile_copy.wait()
-            for copy in panel_copies:
-                copy.start()
 
         for d in range(span):
 
             def add(k):
-                s = lax.rem(landing[k], col_tiles) - per_col
+                s = lax.rem(landing[k], col_tiles)
                 buf[slot, s, d] = buf[slot, s, d] + tiles[k].astype(jnp.float32)
                 return following[k]
 
             lax.while_loop(lambda k: k >= 0, add, head[i * span + d])
 
-        for s in range(wide):
+        for s in range(col_tiles):
             write(i, slot, s).start()
         return 0
 
     lax.fori_loop(0, steps, step, 0)
     for i in range(max(0, steps - depth), steps):
-        for s in range(wide):
+        for s in range(col_tiles):
             write(0, i % depth, s).wait()
-    for copy in panel_copies:
-        copy.wait()
-
-
-def update(landing, front, panel, left, right, arrived, per_col):
+
+
+def update(landing, place, front, panel, arrived, left, right, sub_count, per_col):
     row_tiles, t, col_tiles, _ = front.shape
-    sub_count = right.shape[0]
     span = 2 if row_tiles % 2 == 0 else 1
     depth = 3
     wide = col_tiles - per_col
-    together = 2 if wide % 2 == 0 else 1
+    together = max(d for d in range(1, 11) if wide % d == 0)
+    width = left[0].shape[-1]
     any_spec = pl.BlockSpec(memory_space=ANY)
+    smem = pl.BlockSpec(memory_space=pltpu.SMEM)
     return pl.pallas_call(
         functools.partial(
-            update_kernel, per_col=per_col, sub_count=sub_count, span=span, depth=depth, together=together
+            update_kernel,
+            per_col=per_col,
+            sub_count=sub_count,
+            span=span,
+            depth=depth,
+            together=together,
+            lines=len(left),
+            rounds=len(right) // sub_count,
         ),
-        in_specs=[pl.BlockSpec(memory_space=pltpu.SMEM)] + [any_spec] * 5,
+        in_specs=[smem, smem] + [any_spec] * (3 + len(left) + len(right)),
         out_specs=any_spec,
         out_shape=jax.ShapeDtypeStruct(front.shape, jnp.float32),
         scratch_shapes=[
-            pltpu.VMEM((depth, wide, span, t, t), jnp.float32),
-            pltpu.VMEM(left.shape, left.dtype),
-            pltpu.VMEM((wide, t, left.shape[-1]), right.dtype),
+            pltpu.VMEM((depth, col_tiles, span, t, t), jnp.float32),
+            pltpu.VMEM((row_tiles, t, width), jnp.bfloat16),
+            pltpu.VMEM((wide, t, width), jnp.bfloat16),
             pltpu.VMEM(arrived.shape, arrived.dtype),
             pltpu.SMEM((row_tiles,), jnp.int32),
             pltpu.SMEM(landing.shape, jnp.int32),
             pltpu.SemaphoreType.DMA((depth,)),
             pltpu.SemaphoreType.DMA((depth,)),
             pltpu.SemaphoreType.DMA,
-            pltpu.SemaphoreType.DMA((wide // together,)),
-            pltpu.SemaphoreType.DMA,
-            pltpu.SemaphoreType.DMA((per_col,)),
+            pltpu.SemaphoreType.DMA,
+            pltpu.SemaphoreType.DMA,
         ],
         compiler_params=params(),
         cost_estimate=pl.CostEstimate(
-            flops=2 * row_tiles * t * wide * t * left.shape[-1],
-            bytes_accessed=2 * front.size * 4,
-            transcendentals=0,
+            flops=2 * row_tiles * t * wide * t * width, bytes_accessed=2 * front.size * 4, transcendentals=0
         ),
         name="trailing_update",
-    )(landing, front, panel, left, right, arrived)
-
-
-def across_rows(mine, row_index, col_index, row_count, col_count):
-    if row_count != 4 or col_count != 4:
-        return lax.psum(jnp.where(row_index == col_index, mine, jnp.zeros_like(mine)), "row")
+    )(landing, place, front, panel, arrived, *left, *right)
+
+
+def tie(*values):
+    return lax.optimization_barrier(values)
+
+
+def nearest_first(c, count):
+    return sorted(range(count), key=lambda k: (abs(k - c), k))
+
+
+def exchange(own, row_index, col_index, row_count, col_count, sub_count):
+    half = own.shape[0] // 2
+    spread = row_count == 4 and col_count == 4 and half > 0
     role = row_index ^ col_index
-    half = mine.shape[0] // 2
-    first, second = mine[:half], mine[half:]
+    orders = [nearest_first(c, col_count) for c in range(col_count)]
+    up, down, right = [own], [own], []
+
+    def along(value, step, first, last):
+        pairs = [(c, c + step) for c in range(first, last) if 0 <= c + step < col_count]
+        return lax.ppermute(value, "col", pairs)
 
     def hop(value, moves):
         pairs = []
@@ -405,13 +441,38 @@
                 pairs.append(((c ^ a) * col_count + c, (c ^ b) * col_count + c))
         return lax.ppermute(value, ("row", "col"), pairs)
 
-    first_1 = hop(first, [(0, 1)])
-    second_1 = hop(second, [(0, 2)])
-    first_2 = hop(jnp.where(role == 0, first, first_1), [(0, 2), (1, 3)])
-    second_2 = hop(jnp.where(role == 0, second, second_1), [(0, 1), (2, 3)])
-    first = jnp.where(role == 0, first, jnp.where(role == 1, first_1, first_2))
-    second = jnp.where(role == 0, second, jnp.where(role == 2, second_1, second_2))
-    return jnp.concatenate([first, second], 0)
+    for n in range(col_count):
+        source = own
+        if n > 0:
+            for c in range(col_count):
+                k = orders[c][n]
+                piece = up[c - k] if k < c else down[k - c]
+                source = piece if c == 0 else jnp.where(col_index == c, piece, source)
+        lines = []
+        if n + 1 < col_count:
+            lines = [along(up[n], 1, n, col_count), along(down[n], -1, 0, col_count - n)]
+        if spread:
+            first, second = source[:half], source[half:]
+            first_1, second_1 = tie(hop(first, [(0, 1)]), hop(second, [(0, 2)]))
+            first_2 = hop(jnp.where(role == 0, first, first_1), [(0, 2), (1, 3)])
+            second_2 = hop(jnp.where(role == 0, second, second_1), [(0, 1), (2, 3)])
+            first_2, second_2, *lines = tie(first_2, second_2, *lines)
+            whole = jnp.concatenate(
+                [
+                    jnp.where(role == 0, first, jnp.where(role == 1, first_1, first_2)),
+                    jnp.where(role == 0, second, jnp.where(role == 2, second_1, second_2)),
+                ],
+                0,
+            )
+        else:
+            whole = lax.psum(jnp.where(row_index == col_index, source, jnp.zeros_like(source)), "row")
+        if lines:
+            up.append(lines[0])
+            down.append(lines[1])
+        right.append(whole)
+        for i in range(1, sub_count):
+            right.append(lax.ppermute(whole, "sub", [(s, (s + i) % sub_count) for s in range(sub_count)]))
+    return up, down[1:], right
 
 
 def local(front, child_tiles, tile_owner, tile_slot):
@@ -432,6 +493,7 @@
     group_id = sub_index * row_count + row_index
 
     corner = local_front[0, :, :per_col, :].transpose(1, 0, 2)
+    corner, child_tiles = tie(corner, child_tiles)
     corner = lax.all_gather(corner, ("sub", "row", "col"), axis=0)
 
     outgoing, targets = pack(tile_owner[:, 0], tile_slot, child_tiles, dev_count, capacity)
@@ -442,6 +504,7 @@
         outgoing.reshape(dev_count, capacity, t, t), ("sub", "row", "col"), split_axis=0, concat_axis=0, tiled=True
     ).reshape(dev_count * capacity, t, t)
     lower, inverse = factor(corner, panel_tiles, per_col, col_count)
+    arrived, landing, lower, inverse = tie(arrived, landing, lower, inverse)
 
     panel = assemble_panel(landing, local_front, arrived, per_col)
     shared = lax.all_to_all(
@@ -453,14 +516,31 @@
     is_leading = group_id < panel_tiles
     upper = jnp.where(jnp.logical_and(is_leading, col_index == 0), leading, solved[0])
     solved = jnp.concatenate([upper[None], solved[1:]], 0)
-    rows = lax.all_gather(solved, "col", axis=0, tiled=True)
-    panel_out = lax.dynamic_index_in_dim(
-        rows.reshape(row_tiles, t, per_col, col_count, t), col_index, 3, keepdims=True
-    ).reshape(row_tiles, 1, t, per_col, 1, t)
-    across = across_rows(rows, row_index, col_index, row_count, col_count)
-    right = lax.all_gather(across, "sub", axis=0)
-    left = jnp.concatenate([jnp.where(is_leading, jnp.zeros_like(rows[:1]), rows[:1]), rows[1:]], 0)
-    result = update(landing, local_front, panel, left, right, arrived, per_col)
+    up, down, right = exchange(solved, row_index, col_index, row_count, col_count, sub_count)
+
+    mine = []
+    for piece in up + down:
+        columns = lax.dynamic_index_in_dim(
+            piece.reshape(part, t, per_col, col_count, t), col_index, 3, keepdims=False
+        )
+        mine.append(columns)
+    ordered = []
+    for k in range(col_count):
+        rows = mine[0]
+        for c in range(col_count):
+            if c != k:
+                rows = jnp.where(col_index == c, mine[c - k] if k < c else mine[col_count - 1 + k - c], rows)
+        ordered.append(rows)
+    panel_out = jnp.concatenate(ordered, 0).reshape(row_tiles, 1, t, per_col, 1, t)
+
+    orders = jnp.array([nearest_first(c, col_count) for c in range(col_count)], jnp.int32)
+    place = jnp.concatenate(
+        [
+            jnp.stack([col_index, sub_index, is_leading.astype(jnp.int32)]).astype(jnp.int32),
+            lax.dynamic_index_in_dim(orders, col_index, 0, keepdims=False),
+        ]
+    )
+    result = update(landing, place, local_front, panel, arrived, up + down, right, sub_count, per_col)
     return (result.reshape(front.shape), panel_out)
 
 

time: 857 us -> 508 us (0.59)
  waiting for transfers between devices: 455 us -> 207 us
  Pallas kernels: 289 us -> 127 us
  starting transfers between devices: 25.4 us -> 70.7 us
  local copies, waits for them, and re-layouts: 30.8 us -> 42.3 us
    all_to_all x1, waiting for transfers between devices: 197 us -> 17.9 us  [local(): lax.all_to_all(outgoing.reshape(dev_count, capacity, t, t), ('sub', 'row'...]
    ppermute x4 -> x16, waiting for transfers between devices: 173 us -> 36.9 us  [hop(): return lax.ppermute(value, ('row', 'col'), pairs)]
    pallas_call x1, Pallas kernels: 130 us -> 5.4 us  [pack(): pl.pallas_call(functools.partial(pack_kernel, capacity=capacity), in_spec...]
    all_gather x1, waiting for transfers between devices: 0.01 us -> 102 us  [local(): corner = lax.all_gather(corner, ('sub', 'row', 'col'), axis=0)]
    all_gather x2 -> x0, waiting for transfers between devices: 84.4 us -> none  [the longest x1 80.7 us: local(): rows = lax.all_gather(solved, 'col', axis=0, tiled=True)]
    all_to_all x1, waiting for transfers between devices: 0.01 us -> 48.7 us  [local(): lax.all_to_all(panel.reshape(col_count, part, per_col, t, t), 'col', spli...]
    pallas_call x1, Pallas kernels: 78.4 us -> 40.8 us  [update(): pl.pallas_call(functools.partial(update_kernel, per_col=per_col, sub_coun...]
    ppermute x4 -> x16, starting transfers between devices: 13.3 us -> 46.8 us  [hop(): return lax.ppermute(value, ('row', 'col'), pairs)]
  transfers between devices with their start and end apart: 9 -> 29, of which waited for: 7 -> 16; matrix products, arithmetic and copies ran while one was open for 2% -> 9% of each run, Pallas kernels for 9% -> 16%
where the time goes in v2:
time: 508 us; the launch traced here: 506 us
  waiting for transfers between devices  207 us (41%)
  Pallas kernels  127 us (25%)
  starting transfers between devices  70.7 us (14%)
  local copies, waits for them, and re-layouts  42.3 us (8%)
  other arithmetic  21.9 us (4%)
  between operations  14.6 us (3%)
  blocking collectives  14.3 us (3%)
  matrix products  8.68 us (2%)
    all_gather x1, waiting for transfers between devices, local(): corner = lax.all_gather(corner, ('sub', 'row', 'col'), axis=0)  102 us
    pallas_call x1, Pallas kernels, factor(): pl.pallas_call(functools.partial(factor_kernel, tiles=tiles, per_col=per_...  75.4 us
    all_to_all x1, waiting for transfers between devices, local(): lax.all_to_all(panel.reshape(col_count, part, per_col, t, t), 'col', spli...  48.7 us
    ppermute x16, starting transfers between devices, hop(): return lax.ppermute(value, ('row', 'col'), pairs)  46.8 us
    pallas_call x1, Pallas kernels, update(): pl.pallas_call(functools.partial(update_kernel, per_col=per_col, sub_coun...  40.8 us
    ppermute x16, waiting for transfers between devices, hop(): return lax.ppermute(value, ('row', 'col'), pairs)  36.9 us
    all_to_all x1, waiting for transfers between devices, local(): lax.all_to_all(outgoing.reshape(dev_count, capacity, t, t), ('sub', 'row'...  17.9 us
    all_to_all x1, blocking collectives, local(): lax.all_to_all(targets.reshape(dev_count, capacity), ('sub', 'row', 'col'...  14.3 us
  transfers between devices with their start and end apart: 29, of which 16 were waited for; matrix products, arithmetic and copies ran while one was open for 9% of the time, Pallas kernels for 16%

profile of v2, /device:TPU:0, one launch (start us, length us, event | category | flops | bytes accessed | tf_op | source)
XLA Modules:
  0.0 506.2 jit_solution(11200253020390302744)
XLA Ops:
  9.0 5.4 %pack_children.1 = (bf16[256,128,128]{2,1,0:T(8,128)(2,1)}, s32[256]{0:T(256)}) custom-call(s32[128]{0:T(128)} %bitcast.86, s32[128]{0:T(128)} %slot.1, bf16[128,128,128]{2,1,0:T(8,128)(2,1)} %tiles), custom_call_target="tpu_custom_call" | custom-call | bytes 8388608 | tf_op jit(solution)/shard_map/pack_children/pallas_call | solution.py:55
  15.1 14.3 %all_to_all.19 = s32[32,1,8]{2,1,0:T(1,128)S(1)} all-to-all(s32[32,1,8]{2,1,0:T(1,128)S(1)} %bitcast.85), channel_id=1, replica_groups=mesh['sub'=2,'row'=4,'col'=4] {'sub','row','col'}, dimensions={0} | all-to-all | bytes 2048 | tf_op jit(solution)/shard_map/all_to_all | solution.py:500
  29.4 3.7 all-to-all-start
  34.8 102.1 %all-gather.3.cloned.1.call-done = f32[64,128,128]{2,1,0:T(8,128)} async-done(((f32[2,128,128]{2,1,0:T(8,128)}), f32[64,128,128]{2,1,0:T(8,128)}) %all-gather.3.cloned.1.call-update) | async-done | bytes 4194320 | tf_op jit(solution)/shard_map/all_gather | solution.py:497
  137.0 75.4 %factor_corner.1 = (bf16[1024,1024]{1,0:T(8,128)(2,1)}, f32[1024,1024]{1,0:T(8,128)}) custom-call(f32[32,2,128,128]{3,2,1,0:T(8,128)} %bitcast.87), custom_call_target="tpu_custom_call" | custom-call | flops 99999997952 | bytes 200000000 | tf_op jit(solution)/shard_map/factor_corner/pallas_call | solution.py:163
  212.4 17.9 %all-to-all-done = bf16[32,8,128,128]{3,2,1,0:T(8,128)(2,1)} async-done(((bf16[32,8,128,128]{3,2,1,0:T(8,128)(2,1)}), bf16[32,8,128,128]{3,2,1,0:T(8,128)(2,1)}, u32[]{:S(2)}, u32[]{:S(2)}) %all-to-all-start) | async-done | bytes 8388640 | tf_op jit(solution)/shard_map/all_to_all | solution.py:503
  230.3 4.9 assemble_panel.1.panel
  235.2 4.5 copy.23
  239.8 8.7 %all-to-all-start.2 = ((f32[4,4,2,128,128]{4,2,3,1,0:T(2,128)}), f32[4,4,2,128,128]{4,2,3,1,0:T(2,128)S(1)}, u32[]{:S(2)}, u32[]{:S(2)}) async-start(f32[4,4,2,128,128]{4,2,3,1,0:T(2,128)} %copy.23), calls=%async_computation.2 | async-start | bytes 4194304 | tf_op jit(solution)/shard_map/all_to_all | solution.py:510
  248.5 48.7 %all-to-all-done.2 = f32[4,4,2,128,128]{4,2,3,1,0:T(2,128)S(1)} async-done(((f32[4,4,2,128,128]{4,2,3,1,0:T(2,128)}), f32[4,4,2,128,128]{4,2,3,1,0:T(2,128)S(1)}, u32[]{:S(2)}, u32[]{:S(2)}) %all-to-all-start.2) | async-done | bytes 2097184 | tf_op jit(solution)/shard_map/all_to_all | solution.py:510
  301.9 8.7 %convolution_convert_fusion = bf16[512,1024]{1,0:T(8,128)(2,1)S(1)} fusion(f32[512,1024]{1,0:T(8,128)S(1)} %reshape.66, f32[1024,1024]{1,0:T(8,128)} %get-tuple-element.43), kind=kOutput, calls=%fused_computation.2 | convolution fusion | flops 6442975232 | bytes 7340032 | tf_op jit(solution)/shard_map/dot_general | solution.py:21
  319.9 4.6 collective-permute-start.4
  330.6 4.1 collective-permute-start.3
  334.7 4.2 collective-permute-start.2
  338.9 5.2 %collective-permute-done.3 = bf16[2,128,1024]{2,1,0:T(8,128)(2,1)} collective-permute-done((bf16[2,128,1024]{2,1,0:T(8,128)(2,1)}, bf16[2,128,1024]{2,1,0:T(8,128)(2,1)}, u32[]{:S(2)}, u32[]{:S(2)}) %collective-permute-start.3) | collective-permute-done | bytes 524320 | tf_op jit(solution)/shard_map/ppermute | solution.py:442
  344.1 4.2 collective-permute-done.2
  348.5 4.4 collective-permute-start.7
  356.4 5.5 %collective-permute-done.7 = bf16[2,128,1024]{2,1,0:T(8,128)(2,1)S(1)} collective-permute-done((bf16[2,128,1024]{2,1,0:T(8,128)(2,1)S(1)}, bf16[2,128,1024]{2,1,0:T(8,128)(2,1)S(1)}, u32[]{:S(2)}, u32[]{:S(2)}) %collective-permute-start.7) | collective-permute-done | bytes 524320 | tf_op jit(solution)/shard_map/ppermute | solution.py:442
  363.3 4.4 collective-permute-start.9
  369.1 6.7 %collective-permute-done.9 = bf16[2,128,1024]{2,1,0:T(8,128)(2,1)S(1)} collective-permute-done((bf16[2,128,1024]{2,1,0:T(8,128)(2,1)S(1)}, bf16[2,128,1024]{2,1,0:T(8,128)(2,1)S(1)}, u32[]{:S(2)}, u32[]{:S(2)}) %collective-permute-start.9) | collective-permute-done | bytes 524320 | tf_op jit(solution)/shard_map/ppermute | solution.py:442
  380.9 3.3 collective-permute-start.13
  395.6 5.2 %collective-permute-start.15 = (bf16[2,128,1024]{2,1,0:T(8,128)(2,1)}, bf16[2,128,1024]{2,1,0:T(8,128)(2,1)}, u32[]{:S(2)}, u32[]{:S(2)}) collective-permute-start(bf16[2,128,1024]{2,1,0:T(8,128)(2,1)} %get-tuple-element.87), channel_id=1, source_target_pairs={{0,4},{8,12},{5,1},{13,9},{10,14},{2,6},{15,11},{7,3},{16,20},{24,... | collective-permute-start | bytes 1572872 | tf_op jit(solution)/shard_map/ppermute | solution.py:442
  425.9 5.2 %collective-permute-start.24 = (bf16[2,128,1024]{2,1,0:T(8,128)(2,1)}, bf16[2,128,1024]{2,1,0:T(8,128)(2,1)}, u32[]{:S(2)}, u32[]{:S(2)}) collective-permute-start(bf16[2,128,1024]{2,1,0:T(8,128)(2,1)} %get-tuple-element.79), channel_id=1, source_target_pairs={{0,4},{8,12},{5,1},{13,9},{10,14},{2,6},{15,11},{7,3},{16,20},{24,... | collective-permute-start | bytes 1572872 | tf_op jit(solution)/shard_map/ppermute | solution.py:442
  458.5 40.8 %trailing_update.1 = f32[16,128,32,128]{3,2,1,0:T(8,128)} custom-call(s32[256]{0:T(256)} %reshape.64.landing, s32[7]{0:T(128)} %pad_add_fusion.place, f32[16,128,32,128]{3,2,1,0:T(8,128)} %bitcast.72, f32[16,2,128,128]{3,2,1,0:T(8,128)} %assemble_panel.1.panel, bf16[256,128,128]{2,1,0:T(8,128)(2,1)} %bitcast.5.arrived, ...), custom_call_target="tpu_custom_call" | custom-call | flops 16106127360 | bytes 67108864 | tf_op jit(solution)/shard_map/trailing_update/pallas_call | solution.py:383
  (154 shorter events, 99.5 us)
Async XLA Ops:
  7.2 129.8 %all-gather.3.cloned.1.call-start = ((), (), s32[]{:S(2)}) async-start(), calls=%async_computation.3 | async-start | bytes 4325376 | tf_op jit(solution)/shard_map/all_gather | solution.py:497
  29.4 200.9 %all-to-all-start = ((bf16[32,8,128,128]{3,2,1,0:T(8,128)(2,1)}), bf16[32,8,128,128]{3,2,1,0:T(8,128)(2,1)}, u32[]{:S(2)}, u32[]{:S(2)}) async-start(bf16[32,8,128,128]{3,2,1,0:T(8,128)(2,1)} %bitcast.83), calls=%async_computation | async-start | bytes 16777216 | tf_op jit(solution)/shard_map/all_to_all | solution.py:503
  239.8 57.4 %all-to-all-start.2 = ((f32[4,4,2,128,128]{4,2,3,1,0:T(2,128)}), f32[4,4,2,128,128]{4,2,3,1,0:T(2,128)S(1)}, u32[]{:S(2)}, u32[]{:S(2)}) async-start(f32[4,4,2,128,128]{4,2,3,1,0:T(2,128)} %copy.23), calls=%async_computation.2 | async-start | bytes 4194304 | tf_op jit(solution)/shard_map/all_to_all | solution.py:510
  313.4 12.4 %collective-permute-start = (bf16[2,128,1024]{2,1,0:T(8,128)(2,1)}, bf16[2,128,1024]{2,1,0:T(8,128)(2,1)}, u32[]{:S(2)}, u32[]{:S(2)}) collective-permute-start(bf16[2,128,1024]{2,1,0:T(8,128)(2,1)} %fusion.1), channel_id=1, source_target_pairs={{0,4},{5,1},{10,14},{15,11},{16,20},{21,17},{26,30},{31,27}} | collective-permute-start | bytes 1572872 | tf_op jit(solution)/shard_map/ppermute | solution.py:442
  315.5 12.4 %collective-permute-start.1 = (bf16[2,128,1024]{2,1,0:T(8,128)(2,1)}, bf16[2,128,1024]{2,1,0:T(8,128)(2,1)}, u32[]{:S(2)}, u32[]{:S(2)}) collective-permute-start(bf16[2,128,1024]{2,1,0:T(8,128)(2,1)} %bitcast.16), channel_id=1, source_target_pairs={{0,8},{5,13},{10,2},{15,7},{16,24},{21,29},{26,18},{31,23}} | collective-permute-start | bytes 1572872 | tf_op jit(solution)/shard_map/ppermute | solution.py:442
  318.6 29.6 %collective-permute-start.5 = (bf16[4,128,1024]{2,1,0:T(8,128)(2,1)}, bf16[4,128,1024]{2,1,0:T(8,128)(2,1)S(1)}, u32[]{:S(2)}, u32[]{:S(2)}) collective-permute-start(bf16[4,128,1024]{2,1,0:T(8,128)(2,1)} %pad_maximum_fusion.rest_0_), channel_id=1, source_target_pairs={{1,0},{2,1},{3,2},{5,4},{6,5},{7,6},{9,8},{10,9},{11,10},{13,12},{... | collective-permute-start | bytes 3145736 | tf_op jit(solution)/shard_map/ppermute | solution.py:435
  319.9 28.4 %collective-permute-start.4 = (bf16[4,128,1024]{2,1,0:T(8,128)(2,1)}, bf16[4,128,1024]{2,1,0:T(8,128)(2,1)S(1)}, u32[]{:S(2)}, u32[]{:S(2)}) collective-permute-start(bf16[4,128,1024]{2,1,0:T(8,128)(2,1)} %pad_maximum_fusion.rest_0_), channel_id=1, source_target_pairs={{0,1},{1,2},{2,3},{4,5},{5,6},{6,7},{8,9},{9,10},{10,11},{12,13},{... | collective-permute-start | bytes 3145736 | tf_op jit(solution)/shard_map/ppermute | solution.py:435
  330.6 13.5 %collective-permute-start.3 = (bf16[2,128,1024]{2,1,0:T(8,128)(2,1)}, bf16[2,128,1024]{2,1,0:T(8,128)(2,1)}, u32[]{:S(2)}, u32[]{:S(2)}) collective-permute-start(bf16[2,128,1024]{2,1,0:T(8,128)(2,1)} %broadcast_select_fusion.6), channel_id=1, source_target_pairs={{0,4},{8,12},{5,1},{13,9},{10,14},{2,6},{15,11},{7,3},{16,20},{24,... | collective-permute-start | bytes 1572872 | tf_op jit(solution)/shard_map/ppermute | solution.py:442
  334.7 13.6 %collective-permute-start.2 = (bf16[2,128,1024]{2,1,0:T(8,128)(2,1)}, bf16[2,128,1024]{2,1,0:T(8,128)(2,1)}, u32[]{:S(2)}, u32[]{:S(2)}) collective-permute-start(bf16[2,128,1024]{2,1,0:T(8,128)(2,1)} %broadcast_select_fusion.7), channel_id=1, source_target_pairs={{0,8},{4,12},{5,13},{1,9},{10,2},{14,6},{15,7},{11,3},{16,24},{20,... | collective-permute-start | bytes 1572872 | tf_op jit(solution)/shard_map/ppermute | solution.py:442
  348.5 13.3 %collective-permute-start.7 = (bf16[2,128,1024]{2,1,0:T(8,128)(2,1)S(1)}, bf16[2,128,1024]{2,1,0:T(8,128)(2,1)S(1)}, u32[]{:S(2)}, u32[]{:S(2)}) collective-permute-start(bf16[2,128,1024]{2,1,0:T(8,128)(2,1)S(1)} %get-tuple-element.93), channel_id=1, source_target_pairs={{0,8},{5,13},{10,2},{15,7},{16,24},{21,29},{26,18},{31,23}} | collective-permute-start | bytes 1572872 | tf_op jit(solution)/shard_map/ppermute | solution.py:442
  354.3 22.8 %collective-permute-start.10 = (bf16[4,128,1024]{2,1,0:T(8,128)(2,1)}, bf16[4,128,1024]{2,1,0:T(8,128)(2,1)S(1)}, u32[]{:S(2)}, u32[]{:S(2)}) collective-permute-start(bf16[4,128,1024]{2,1,0:T(8,128)(2,1)} %copy-done.8), channel_id=1, source_target_pairs={{1,2},{2,3},{5,6},{6,7},{9,10},{10,11},{13,14},{14,15},{17,18},{18... | collective-permute-start | bytes 3145736 | tf_op jit(solution)/shard_map/ppermute | solution.py:435
  355.1 24.4 %collective-permute-start.11 = (bf16[4,128,1024]{2,1,0:T(8,128)(2,1)S(1)}, bf16[4,128,1024]{2,1,0:T(8,128)(2,1)}, u32[]{:S(2)}, u32[]{:S(2)}) collective-permute-start(bf16[4,128,1024]{2,1,0:T(8,128)(2,1)S(1)} %collective-permute-done.5.rest_4_), channel_id=1, source_target_pairs={{1,0},{2,1},{5,4},{6,5},{9,8},{10,9},{13,12},{14,13},{17,16},{18,1... | collective-permute-start | bytes 3145736 | tf_op jit(solution)/shard_map/ppermute | solution.py:435
  363.3 12.4 %collective-permute-start.9 = (bf16[2,128,1024]{2,1,0:T(8,128)(2,1)S(1)}, bf16[2,128,1024]{2,1,0:T(8,128)(2,1)S(1)}, u32[]{:S(2)}, u32[]{:S(2)}) collective-permute-start(bf16[2,128,1024]{2,1,0:T(8,128)(2,1)S(1)} %get-tuple-element.91), channel_id=1, source_target_pairs={{0,4},{8,12},{5,1},{13,9},{10,14},{2,6},{15,11},{7,3},{16,20},{24,... | collective-permute-start | bytes 1572872 | tf_op jit(solution)/shard_map/ppermute | solution.py:442
  380.9 10.4 %collective-permute-start.13 = (bf16[2,128,1024]{2,1,0:T(8,128)(2,1)S(1)}, bf16[2,128,1024]{2,1,0:T(8,128)(2,1)S(1)}, u32[]{:S(2)}, u32[]{:S(2)}) collective-permute-start(bf16[2,128,1024]{2,1,0:T(8,128)(2,1)S(1)} %get-tuple-element.89), channel_id=1, source_target_pairs={{0,8},{5,13},{10,2},{15,7},{16,24},{21,29},{26,18},{31,23}} | collective-permute-start | bytes 1572872 | tf_op jit(solution)/shard_map/ppermute | solution.py:442
  386.0 26.8 %collective-permute-start.16 = (bf16[4,128,1024]{2,1,0:T(8,128)(2,1)S(1)}, bf16[4,128,1024]{2,1,0:T(8,128)(2,1)}, u32[]{:S(2)}, u32[]{:S(2)}) collective-permute-start(bf16[4,128,1024]{2,1,0:T(8,128)(2,1)S(1)} %collective-permute-done.10.rest_2_), channel_id=1, source_target_pairs={{2,3},{6,7},{10,11},{14,15},{18,19},{22,23},{26,27},{30,31}} | collective-permute-start | bytes 3145736 | tf_op jit(solution)/shard_map/ppermute | solution.py:435
  387.7 25.2 %collective-permute-start.17 = (bf16[4,128,1024]{2,1,0:T(8,128)(2,1)}, bf16[4,128,1024]{2,1,0:T(8,128)(2,1)}, u32[]{:S(2)}, u32[]{:S(2)}) collective-permute-start(bf16[4,128,1024]{2,1,0:T(8,128)(2,1)} %collective-permute-done.11.rest_5_), channel_id=1, source_target_pairs={{1,0},{5,4},{9,8},{13,12},{17,16},{21,20},{25,24},{29,28}} | collective-permute-start | bytes 3145736 | tf_op jit(solution)/shard_map/ppermute | solution.py:435
  395.6 17.3 %collective-permute-start.15 = (bf16[2,128,1024]{2,1,0:T(8,128)(2,1)}, bf16[2,128,1024]{2,1,0:T(8,128)(2,1)}, u32[]{:S(2)}, u32[]{:S(2)}) collective-permute-start(bf16[2,128,1024]{2,1,0:T(8,128)(2,1)} %get-tuple-element.87), channel_id=1, source_target_pairs={{0,4},{8,12},{5,1},{13,9},{10,14},{2,6},{15,11},{7,3},{16,20},{24,... | collective-permute-start | bytes 1572872 | tf_op jit(solution)/shard_map/ppermute | solution.py:442
  400.7 12.1 %collective-permute-start.14 = (bf16[2,128,1024]{2,1,0:T(8,128)(2,1)}, bf16[2,128,1024]{2,1,0:T(8,128)(2,1)}, u32[]{:S(2)}, u32[]{:S(2)}) collective-permute-start(bf16[2,128,1024]{2,1,0:T(8,128)(2,1)} %get-tuple-element.88), channel_id=1, source_target_pairs={{0,8},{4,12},{5,13},{1,9},{10,2},{14,6},{15,7},{11,3},{16,24},{20,... | collective-permute-start | bytes 1572872 | tf_op jit(solution)/shard_map/ppermute | solution.py:442
  420.2 38.3 %collective-permute-start.18 = (bf16[4,128,1024]{2,1,0:T(8,128)(2,1)}, bf16[4,128,1024]{2,1,0:T(8,128)(2,1)}, u32[]{:S(2)}, u32[]{:S(2)}) collective-permute-start(bf16[4,128,1024]{2,1,0:T(8,128)(2,1)} %pad_maximum_fusion.1.rest_7_), channel_id=1, source_target_pairs={{0,16},{16,0},{1,17},{17,1},{2,18},{18,2},{3,19},{19,3},{4,20},{20... | collective-permute-start | bytes 3145736 | tf_op jit(solution)/shard_map/ppermute | solution.py:474
  425.9 15.6 %collective-permute-start.24 = (bf16[2,128,1024]{2,1,0:T(8,128)(2,1)}, bf16[2,128,1024]{2,1,0:T(8,128)(2,1)}, u32[]{:S(2)}, u32[]{:S(2)}) collective-permute-start(bf16[2,128,1024]{2,1,0:T(8,128)(2,1)} %get-tuple-element.79), channel_id=1, source_target_pairs={{0,4},{8,12},{5,1},{13,9},{10,14},{2,6},{15,11},{7,3},{16,20},{24,... | collective-permute-start | bytes 1572872 | tf_op jit(solution)/shard_map/ppermute | solution.py:442
  431.1 10.4 %collective-permute-start.23 = (bf16[2,128,1024]{2,1,0:T(8,128)(2,1)}, bf16[2,128,1024]{2,1,0:T(8,128)(2,1)}, u32[]{:S(2)}, u32[]{:S(2)}) collective-permute-start(bf16[2,128,1024]{2,1,0:T(8,128)(2,1)} %get-tuple-element.80), channel_id=1, source_target_pairs={{0,8},{4,12},{5,13},{1,9},{10,2},{14,6},{15,7},{11,3},{16,24},{20,... | collective-permute-start | bytes 1572872 | tf_op jit(solution)/shard_map/ppermute | solution.py:442
  441.5 17.0 %collective-permute-start.19 = (bf16[4,128,1024]{2,1,0:T(8,128)(2,1)}, bf16[4,128,1024]{2,1,0:T(8,128)(2,1)}, u32[]{:S(2)}, u32[]{:S(2)}) collective-permute-start(bf16[4,128,1024]{2,1,0:T(8,128)(2,1)} %pad_maximum_fusion.2.rest_9_), channel_id=1, source_target_pairs={{0,16},{16,0},{1,17},{17,1},{2,18},{18,2},{3,19},{19,3},{4,20},{20... | collective-permute-start | bytes 3145736 | tf_op jit(solution)/shard_map/ppermute | solution.py:474
  443.5 15.0 %collective-permute-start.20 = (bf16[4,128,1024]{2,1,0:T(8,128)(2,1)S(1)}, bf16[4,128,1024]{2,1,0:T(8,128)(2,1)}, u32[]{:S(2)}, u32[]{:S(2)}) collective-permute-start(bf16[4,128,1024]{2,1,0:T(8,128)(2,1)S(1)} %pad_maximum_fusion.3.rest_11_), channel_id=1, source_target_pairs={{0,16},{16,0},{1,17},{17,1},{2,18},{18,2},{3,19},{19,3},{4,20},{20... | collective-permute-start | bytes 3145736 | tf_op jit(solution)/shard_map/ppermute | solution.py:474
  445.2 13.3 %collective-permute-start.25 = (bf16[4,128,1024]{2,1,0:T(8,128)(2,1)}, bf16[4,128,1024]{2,1,0:T(8,128)(2,1)}, u32[]{:S(2)}, u32[]{:S(2)}) collective-permute-start(bf16[4,128,1024]{2,1,0:T(8,128)(2,1)} %pad_maximum_fusion.4.rest_13_), channel_id=1, source_target_pairs={{0,16},{16,0},{1,17},{17,1},{2,18},{18,2},{3,19},{19,3},{4,20},{20... | collective-permute-start | bytes 3145736 | tf_op jit(solution)/shard_map/ppermute | solution.py:474
  (35 other events, 370.1 us)
Sparse Core Ops, SparseCore 0:
  11.6 125.3 all-gather.2

commit v3 on v2

v3 whole, which is shorter than its diff:
```python
import functools

import jax
import jax.numpy as jnp
from jax import lax
from jax.experimental import pallas as pl
from jax.experimental.pallas import tpu as pltpu
from jax.sharding import PartitionSpec as P

NB = 1024
ANY = pl.ANY
EXACT = lax.Precision.HIGHEST
VMEM_LIMIT = 56 * 1024 * 1024


def params():
    return pltpu.CompilerParams(vmem_limit_bytes=VMEM_LIMIT)


def contract(a, b, dim_a, dim_b):
    return lax.dot_general(
        a, b, (((dim_a,), (dim_b,)), ((), ())), precision=EXACT, preferred_element_type=jnp.float32
    )


def pack_kernel(owner, slot, tiles, first, second, targets, counts, held, in_sem, sem, *, cut, per_col, col_tiles):
    tile_count = tiles.shape[0]
    dev_count = counts.shape[0]
    late = second.shape[0] // dev_count
    load = pltpu.make_async_copy(tiles, held, in_sem)
    load.start()

    def clear(d, _):
        counts[d] = 0
        for r in range(cut + late):
            targets[d * (cut + late) + r] = -1
        return 0

    lax.fori_loop(0, dev_count, clear, 0)
    load.wait()

    def send(k, lost, panel):
        chosen = lax.rem(slot[k], col_tiles) < per_col
        chosen = chosen if panel else jnp.logical_not(chosen)
        d = owner[k]
        rank = counts[d]

        @pl.when(chosen)
        def _():
            counts[d] = rank + 1
            targets[d * (cut + late) + rank] = slot[k]

            @pl.when(rank < cut)
            def _():
                pltpu.make_async_copy(held.at[k], first.at[d * cut + rank], sem).start()

            @pl.when(rank >= cut)
            def _():
                pltpu.make_async_copy(held.at[k], second.at[d * late + rank - cut], sem).start()

        return lost + jnp.logical_and(chosen, rank >= cut).astype(jnp.int32)

    targets[dev_count * (cut + late)] = lax.fori_loop(0, tile_count, functools.partial(send, panel=True), 0)
    lax.fori_loop(0, tile_count, functools.partial(send, panel=False), 0)
    pltpu.make_async_copy(held, held, sem).wait()


def pack(owner, slot, tiles, dev_count, cut, late, per_col, col_tiles):
    smem = pl.BlockSpec(memory_space=pltpu.SMEM)
    any_spec = pl.BlockSpec(memory_space=ANY)
    return pl.pallas_call(
        functools.partial(pack_kernel, cut=cut, per_col=per_col, col_tiles=col_tiles),
        in_specs=[smem, smem, any_spec],
        out_specs=[any_spec, any_spec, smem],
        out_shape=[
            jax.ShapeDtypeStruct((dev_count * cut,) + tiles.shape[1:], tiles.dtype),
            jax.ShapeDtypeStruct((dev_count * late,) + tiles.shape[1:], tiles.dtype),
            jax.ShapeDtypeStruct((dev_count * (cut + late) + 1,), jnp.int32),
        ],
        scratch_shapes=[
            pltpu.SMEM((dev_count,), jnp.int32),
            pltpu.VMEM(tiles.shape, tiles.dtype),
            pltpu.SemaphoreType.DMA,
            pltpu.SemaphoreType.DMA,
        ],
        compiler_params=params(),
        cost_estimate=pl.CostEstimate(flops=0, bytes_accessed=20_000_000, transcendentals=0),
        name="pack_children",
    )(owner, slot, tiles)


def eliminate(tile):
    n = tile.shape[0]
    groups = n // 8
    rows = lax.broadcasted_iota(jnp.int32, (8, n), 0)
    lanes = lax.broadcasted_iota(jnp.int32, (8, n), 1)
    upper = [tile[8 * h : 8 * h + 8, :] for h in range(groups)]
    ops = [jnp.where(lanes == rows + 8 * h, 1.0, 0.0).astype(jnp.float32) for h in range(groups)]
    column = [jnp.broadcast_to(upper[h][:, 0:1], (8, n)) for h in range(groups)]
    for j in range(n):
        g, u = divmod(j, 8)
        inverse = 1.0 / column[g][u : u + 1, :]
        row = upper[g][u : u + 1, :] * inverse
        row_ops = ops[g][u : u + 1, :] * inverse
        ahead = [None] * groups
        if j + 1 < n:
            g1, u1 = divmod(j + 1, 8)
            scale = column[g1][u1 : u1 + 1, :] * inverse
            for h in range(g1, groups):
                ahead[h] = jnp.broadcast_to(upper[h][:, j + 1 : j + 2], (8, n)) - column[h] * scale
        for h in range(g, groups):
            below = column[h]
            if h == g:
                below = jnp.where(rows > u, below, 0.0)
            upper[h] = upper[h] - below * row
            ops[h] = ops[h] - below * row_ops
        column = ahead
    return jnp.concatenate(upper, 0), jnp.concatenate(ops, 0)


def factor_kernel(corner, lower, inverse, work, copied, sem, *, tiles, per_col, col_count):
    t = corner.shape[-1]
    rows = lax.broadcasted_iota(jnp.int32, (t, t), 0)
    cols = lax.broadcasted_iota(jnp.int32, (t, t), 1)
    copies = []
    for p in range(tiles):
        for j in range(p + 1):
            copies.append(
                pltpu.make_async_copy(
                    corner.at[p * col_count + j % col_count, j // col_count], copied.at[p, j], sem
                )
            )
    for copy in copies:
        copy.start()
    lower[...] = jnp.zeros_like(lower)
    for copy in copies:
        copy.wait()

    for p in range(tiles):
        for j in range(p + 1):
            block = copied[p, j]
            if p == j:
                block = jnp.where(rows >= cols, block, block.T)
                work[p, :, p * t : (p + 1) * t] = block
            else:
                work[p, :, j * t : (j + 1) * t] = block
                work[j, :, p * t : (p + 1) * t] = block.T

    def step(j, _):
        here = pl.ds(pl.multiple_of(j * t, t), t)
        upper, ops = eliminate(work[j, :, here])
        pivots = jnp.sum(jnp.where(rows == cols, upper, 0.0), 1, keepdims=True)
        scale = lax.rsqrt(pivots)
        upper = jnp.where(rows <= cols, upper * scale, 0.0)
        ops = jnp.where(rows >= cols, ops * scale, 0.0)
        lower[pl.ds(pl.multiple_of(j * t, t), t), here] = upper.T.astype(lower.dtype)
        work[j, :, here] = jnp.where(rows == cols, 1.0, 0.0)
        work[j] = contract(ops, work[j], 1, 0)

        def below(i, _):
            block = contract(work[i, :, here], ops, 1, 1)
            lower[pl.ds(pl.multiple_of(i * t, t), t), here] = block.astype(lower.dtype)
            work[i, :, here] = jnp.zeros((t, t), jnp.float32)
            work[i] = work[i] - contract(block, work[j], 1, 0)
            return 0

        lax.fori_loop(j + 1, tiles, below, 0)
        return 0

    lax.fori_loop(0, tiles, step, 0)
    wide_rows = lax.broadcasted_iota(jnp.int32, (t, tiles * t), 1)
    for p in range(tiles):
        inverse[p * t : (p + 1) * t, :] = jnp.where(wide_rows < (p + 1) * t, work[p], 0.0)


def factor(corner, tiles, per_col, col_count):
    t = corner.shape[-1]
    n = tiles * t
    vmem = pl.BlockSpec(memory_space=pltpu.VMEM)
    return pl.pallas_call(
        functools.partial(factor_kernel, tiles=tiles, per_col=per_col, col_count=col_count),
        in_specs=[pl.BlockSpec(memory_space=ANY)],
        out_specs=[vmem, vmem],
        out_shape=[jax.ShapeDtypeStruct((n, n), jnp.bfloat16), jax.ShapeDtypeStruct((n, n), jnp.float32)],
        scratch_shapes=[
            pltpu.VMEM((tiles, t, n), jnp.float32),
            pltpu.VMEM((tiles, tiles, t, t), jnp.float32),
            pltpu.SemaphoreType.DMA,
        ],
        compiler_params=params(),
        cost_estimate=pl.CostEstimate(flops=100_000_000_000, bytes_accessed=200_000_000, transcendentals=0),
        name="factor_corner",
    )(corner)


def corner_kernel(front, out, held, in_sem, out_sem):
    per_col = out.shape[0]
    copies = [pltpu.make_async_copy(front.at[0, :, s, :], held.at[s], in_sem.at[s]) for s in range(per_col)]
    for copy in copies:
        copy.start()
    for copy in copies:
        copy.wait()
    copy = pltpu.make_async_copy(held, out, out_sem)
    copy.start()
    copy.wait()


def take_corner(front, per_col):
    _, t, _, _ = front.shape
    any_spec = pl.BlockSpec(memory_space=ANY)
    return pl.pallas_call(
        corner_kernel,
        in_specs=[any_spec],
        out_specs=any_spec,
        out_shape=jax.ShapeDtypeStruct((per_col, t, t), front.dtype),
        scratch_shapes=[
            pltpu.VMEM((per_col, t, t), front.dtype),
            pltpu.SemaphoreType.DMA((per_col,)),
            pltpu.SemaphoreType.DMA,
        ],
        compiler_params=params(),
        cost_estimate=pl.CostEstimate(flops=0, bytes_accessed=500_000, transcendentals=0),
        name="take_corner",
    )(front)


def panel_kernel(landing, front, arrived, out, buf, tiles, picked, in_sem, tile_sem, out_sem, *, per_col, col_tiles):
    slots = landing.shape[0]

    def front_copy(s):
        return pltpu.make_async_copy(front.at[:, :, s, :], buf.at[:, s], in_sem)

    for s in range(per_col):
        front_copy(s).start()

    def find(k, n):
        slot = landing[k]
        hit = jnp.logical_and(slot >= 0, lax.rem(slot, col_tiles) < per_col)

        @pl.when(hit)
        def _():
            picked[n] = slot
            pltpu.make_async_copy(arrived.at[k], tiles.at[n], tile_sem).start()

        return n + hit.astype(jnp.int32)

    found = lax.fori_loop(0, slots, find, 0)
    for s in range(per_col):
        front_copy(s).wait()

    def wait(n, _):
        pltpu.make_async_copy(arrived.at[0], tiles.at[0], tile_sem).wait()
        return 0

    lax.fori_loop(0, found, wait, 0)

    def add(n, _):
        q = picked[n] // col_tiles
        s = lax.rem(picked[n], col_tiles)
        buf[q, s] = buf[q, s] + tiles[n].astype(jnp.float32)
        return 0

    lax.fori_loop(0, found, add, 0)
    copy = pltpu.make_async_copy(buf, out, out_sem)
    copy.start()
    copy.wait()


def assemble_panel(landing, front, arrived, per_col):
    row_tiles, t, col_tiles, _ = front.shape
    any_spec = pl.BlockSpec(memory_space=ANY)
    return pl.pallas_call(
        functools.partial(panel_kernel, per_col=per_col, col_tiles=col_tiles),
        in_specs=[pl.BlockSpec(memory_space=pltpu.SMEM), any_spec, any_spec],
        out_specs=any_spec,
        out_shape=jax.ShapeDtypeStruct((row_tiles, per_col, t, t), jnp.float32),
        scratch_shapes=[
            pltpu.VMEM((row_tiles, per_col, t, t), jnp.float32),
            pltpu.VMEM(arrived.shape, arrived.dtype),
            pltpu.SMEM(landing.shape, jnp.int32),
            pltpu.SemaphoreType.DMA,
            pltpu.SemaphoreType.DMA,
            pltpu.SemaphoreType.DMA,
        ],
        compiler_params=params(),
        cost_estimate=pl.CostEstimate(flops=0, bytes_accessed=20_000_000, transcendentals=0),
        name="assemble_panel",
    )(landing, front, arrived)


def solve_kernel(where, inverse, lower, *rest, col_count):
    pieces, rest = rest[:col_count], rest[col_count:]
    solved, rows, inverse_v, lead, sem, inv_sem, lead_sem = rest
    part, per_col, t, _ = pieces[0].shape
    for i in range(col_count):
        origin = where[2 + i]
        for q in range(part):
            for s in range(per_col):
                column = pl.multiple_of((s * col_count + origin) * t, t)
                pltpu.make_async_copy(
                    pieces[i].at[q, s], rows.at[pl.ds(q * t, t), pl.ds(column, t)], sem
                ).start()
    inv_copy = pltpu.make_async_copy(inverse, inverse_v, inv_sem)
    inv_copy.start()
    lead_copy = pltpu.make_async_copy(lower.at[pl.ds(where[1] * t, t)], lead, lead_sem)
    lead_copy.start()
    pltpu.make_async_copy(rows, rows, sem).wait()
    inv_copy.wait()
    lead_copy.wait()
    n = inverse.shape[0]
    step = 2 * t if n % (2 * t) == 0 else t
    for b in range(0, n, step):
        product = contract(rows[:, : b + step], inverse_v[b : b + step, : b + step], 1, 1)
        solved[:, b : b + step] = product.astype(solved.dtype)

    @pl.when(where[0] == 1)
    def _():
        solved[:t, :] = lead[...]


def solve(where, pieces, inverse, lower):
    part, _, t, _ = pieces[0].shape
    n = inverse.shape[0]
    any_spec = pl.BlockSpec(memory_space=ANY)
    return pl.pallas_call(
        functools.partial(solve_kernel, col_count=len(pieces)),
        in_specs=[pl.BlockSpec(memory_space=pltpu.SMEM)] + [any_spec] * (2 + len(pieces)),
        out_specs=pl.BlockSpec(memory_space=pltpu.VMEM),
        out_shape=jax.ShapeDtypeStruct((part * t, n), jnp.bfloat16),
        scratch_shapes=[
            pltpu.VMEM((part * t, n), jnp.float32),
            pltpu.VMEM((n, n), jnp.float32),
            pltpu.VMEM((t, n), jnp.bfloat16),
            pltpu.SemaphoreType.DMA,
            pltpu.SemaphoreType.DMA,
            pltpu.SemaphoreType.DMA,
        ],
        compiler_params=params(),
        cost_estimate=pl.CostEstimate(flops=8_000_000_000, bytes_accessed=12_000_000, transcendentals=0),
        name="solve_rows",
    )(where, inverse, lower, *pieces)


def update_kernel(
    area, spot, place, table, front, arrived, arrived_late, *rest,
    blocks, orders, per_col, sub_count, depth, reach, aliased,
):
    row_used = sorted({i for i, _ in blocks})
    col_used = sorted({j for _, j in blocks})
    ups, rest = rest[:reach], rest[reach:]
    downs, rest = rest[:reach], rest[reach:]
    right, rest = rest[: len(col_used) * sub_count], rest[len(col_used) * sub_count :]
    rest = rest[1:] if aliased else rest
    out, token, buf, left_v, right_v, tiles, picked, head, following, lookup = rest[:10]
    in_sem, out_sem, left_sem, right_sem, tile_sem = rest[10:]
    token[...] = jnp.zeros_like(token)
    early = arrived.shape[0]
    t = front.shape[1]
    slots = area.shape[0]
    steps = len(blocks)
    part = ups[0].shape[0]
    count = len(orders)
    width = part * sub_count

    def corner_of(b):
        return place[3 + table[4 * b]], place[3 + table[4 * b + 1]]

    def read(b, slot):
        rows, cols = corner_of(b)
        for j in range(width):
            source = front.at[pl.ds(rows * part, part), :, cols * width + j, :]
            pltpu.make_async_copy(source, buf.at[slot, j], in_sem.at[slot]).start()

    def write(b, slot):
        rows, cols = corner_of(b)
        for j in range(width):
            target = out.at[pl.ds(rows * part, part), :, cols * width + j, :]
            pltpu.make_async_copy(buf.at[slot, j], target, out_sem.at[slot]).start()

    def drain(slot, sem):
        pltpu.make_async_copy(buf.at[slot], buf.at[slot], sem.at[slot]).wait()

    for n, i in enumerate(row_used):
        for c in range(count):
            k = orders[c][i]

            @pl.when(place[0] == c)
            def _(n=n, c=c, k=k):
                piece = ups[c - k] if k <= c else downs[k - c]
                pltpu.make_async_copy(piece, left_v.at[n], left_sem).start()

    for n in range(len(col_used)):
        for i in range(sub_count):
            origin = lax.rem(place[1] + sub_count - i, sub_count)
            for r in range(part):
                pltpu.make_async_copy(
                    right[n * sub_count + i].at[r], right_v.at[n, r * sub_count + origin], right_sem
                ).start()
    for b in range(min(depth - 1, steps)):
        read(b, b)

    for k in range(count * count + 1):
        lookup[k] = -1
    for b in range(steps):
        head[b] = -1
        rows, cols = corner_of(b)
        lookup[rows * count + cols] = b

    def find(k, n):
        b = lookup[area[k]]
        hit = b >= 0

        @pl.when(hit)
        def _():
            picked[n] = spot[k]
            following[n] = head[b]
            head[b] = n

            @pl.when(k < early)
            def _():
                pltpu.make_async_copy(arrived.at[k], tiles.at[n], tile_sem).start()

            @pl.when(k >= early)
            def _():
                pltpu.make_async_copy(arrived_late.at[k - early], tiles.at[n], tile_sem).start()

        return n + hit.astype(jnp.int32)

    found = lax.fori_loop(0, slots, find, 0)
    pltpu.make_async_copy(left_v, left_v, left_sem).wait()
    for n, i in enumerate(row_used):

        @pl.when(jnp.logical_and(place[2] == 1, place[3 + i] == 0))
        def _(n=n):
            left_v[n, 0] = jnp.zeros_like(left_v[n, 0])

    pltpu.make_async_copy(right_v, right_v, right_sem).wait()
    for n, j in enumerate(col_used):

        @pl.when(place[3 + j] == 0)
        def _(n=n):
            right_v[n, :per_col] = jnp.zeros_like(right_v[n, :per_col])

    def wait_tile(n, _):
        pltpu.make_async_copy(arrived.at[0], tiles.at[0], tile_sem).wait()
        return 0

    lax.fori_loop(0, found, wait_tile, 0)

    def step(b, _):
        slot = lax.rem(b, depth)

        @pl.when(b + depth - 1 < steps)
        def _():
            later = lax.rem(b + depth - 1, depth)

            @pl.when(b >= 1)
            def _():
                drain(later, out_sem)

            read(b + depth - 1, later)

        drain(slot, in_sem)
        rows = left_v[table[4 * b + 2]].reshape(part * t, left_v.shape[-1])
        cols = right_v[table[4 * b + 3]].reshape(width * t, right_v.shape[-1])
        product = lax.dot_general(rows, cols, (((1,), (1,)), ((), ())), preferred_element_type=jnp.float32)
        for j in range(width):
            piece = product[:, j * t : (j + 1) * t].reshape(part, t, t)
            buf[slot, j] = buf[slot, j] - piece

        def add(n):
            j, q = lax.rem(picked[n], width), lax.div(picked[n], width)
            buf[slot, j, q] = buf[slot, j, q] + tiles[n].astype(jnp.float32)
            return following[n]

        lax.while_loop(lambda n: n >= 0, add, head[b])
        write(b, slot)
        return 0

    lax.fori_loop(0, steps, step, 0)
    for b in range(max(0, steps - depth), steps):
        drain(b % depth, out_sem)


def update(area, spot, place, front, arrived, arrived_late, up, down, right, so_far, blocks, orders, per_col):
    t = front.shape[1]
    sub_count = len(right[0])
    part, _, inner = up[0].shape
    width = part * sub_count
    count = len(orders)
    row_used = sorted({i for i, _ in blocks})
    col_used = sorted({j for _, j in blocks})
    depth = min(4, len(blocks))
    reach = len(up)
    any_spec = pl.BlockSpec(memory_space=ANY)
    smem = pl.BlockSpec(memory_space=pltpu.SMEM)
    table = jnp.array([v for i, j in blocks for v in (i, j, row_used.index(i), col_used.index(j))], jnp.int32)
    operands = [area, spot, place, table, front, arrived, arrived_late, *up, *down]
    for j in col_used:
        operands.extend(right[j])
    aliased = so_far is not None
    aliases = {}
    if aliased:
        aliases = {len(operands): 0}
        operands.append(so_far)
    return pl.pallas_call(
        functools.partial(
            update_kernel,
            blocks=tuple(blocks),
            orders=orders,
            per_col=per_col,
            sub_count=sub_count,
            depth=depth,
            reach=reach,
            aliased=aliased,
        ),
        in_specs=[smem] * 4 + [any_spec] * (len(operands) - 4),
        out_specs=[any_spec, pl.BlockSpec(memory_space=pltpu.VMEM)],
        out_shape=[jax.ShapeDtypeStruct(front.shape, jnp.float32), jax.ShapeDtypeStruct((8, 128), jnp.int32)],
        scratch_shapes=[
            pltpu.VMEM((depth, width, part, t, t), jnp.float32),
            pltpu.VMEM((len(row_used), part, t, inner), jnp.bfloat16),
            pltpu.VMEM((len(col_used), width, t, inner), jnp.bfloat16),
            pltpu.VMEM(area.shape + (t, t), arrived.dtype),
            pltpu.SMEM(area.shape, jnp.int32),
            pltpu.SMEM((len(blocks),), jnp.int32),
            pltpu.SMEM(area.shape, jnp.int32),
            pltpu.SMEM((count * count + 1,), jnp.int32),
            pltpu.SemaphoreType.DMA((depth,)),
            pltpu.SemaphoreType.DMA((depth,)),
            pltpu.SemaphoreType.DMA,
            pltpu.SemaphoreType.DMA,
            pltpu.SemaphoreType.DMA,
        ],
        input_output_aliases=aliases,
        compiler_params=params(),
        cost_estimate=pl.CostEstimate(
            flops=2 * len(blocks) * part * t * width * t * inner,
            bytes_accessed=2 * len(blocks) * part * t * width * t * 4,
            transcendentals=0,
        ),
        name="update_blocks",
    )(*operands)


def tie(*values):
    return lax.optimization_barrier(values)


def nearest_first(c, count):
    return sorted(range(count), key=lambda k: (abs(k - c), k))


def exchange(own, late, update_with, so_far, indices, counts):
    _, row_index, col_index = indices
    sub_count, row_count, col_count = counts
    half = own.shape[0] // 2
    spread = row_count == 4 and col_count == 4 and half > 0
    role = row_index ^ col_index
    orders = [nearest_first(c, col_count) for c in range(col_count)]
    up, down, right = [own], [own], []
    done = set()

    def along(value, step, first, last):
        pairs = [(c, c + step) for c in range(first, last) if 0 <= c + step < col_count]
        return lax.ppermute(value, "col", pairs)

    def hop(value, moves):
        pairs = []
        for c in range(col_count):
            for a, b in moves:
                pairs.append(((c ^ a) * col_count + c, (c ^ b) * col_count + c))
        return lax.ppermute(value, ("row", "col"), pairs)

    def advance(so_far, value, most):
        ready = [(i, j) for j in range(len(right)) for i in range(min(len(up), col_count)) if (i, j) not in done]
        ready = ready[:most]
        if not ready:
            return so_far, value
        done.update(ready)
        so_far, token = update_with(late, up, down, right, so_far, ready, orders)
        return so_far, value + token[0, 0]

    batch = col_count * (col_count - 2)
    for n in range(col_count):
        source = own
        if n > 0:
            for c in range(col_count):
                k = orders[c][n]
                piece = up[c - k] if k < c else down[k - c]
                source = piece if c == 0 else jnp.where(col_index == c, piece, source)
        lines = []
        if n + 1 < col_count:
            lines = [along(up[n], 1, n, col_count), along(down[n], -1, 0, col_count - n)]
        busy = spread and n + 1 == col_count
        known = role
        if spread:
            first, second = source[:half], source[half:]
            first_1, second_1 = tie(hop(first, [(0, 1)]), hop(second, [(0, 2)]))
            if busy:
                so_far, known = advance(so_far, known, batch)
            first_2 = hop(jnp.where(known == 0, first, first_1), [(0, 2), (1, 3)])
            second_2 = hop(jnp.where(known == 0, second, second_1), [(0, 1), (2, 3)])
            if n == 0:
                first_2, second_2, late, *lines = tie(first_2, second_2, late, *lines)
            else:
                first_2, second_2, *lines = tie(first_2, second_2, *lines)
            if busy:
                so_far, known = advance(so_far, known, batch)
            whole = jnp.concatenate(
                [
                    jnp.where(known == 0, first, jnp.where(known == 1, first_1, first_2)),
                    jnp.where(known == 0, second, jnp.where(known == 2, second_1, second_2)),
                ],
                0,
            )
        else:
            whole = lax.psum(jnp.where(row_index == col_index, source, jnp.zeros_like(source)), "row")
        if lines:
            up.append(lines[0])
            down.append(lines[1])
        right.append(
            [whole]
            + [lax.ppermute(whole, "sub", [(s, (s + i) % sub_count) for s in range(sub_count)]) for i in range(1, sub_count)]
        )
    while len(done) < col_count * col_count:
        so_far, _ = advance(so_far, role, col_count * col_count)
    return so_far, up + down[1:]


def panel_columns(pieces, col_index, col_count, per_col):
    part, t, width = pieces[0].shape
    mine = []
    for piece in pieces:
        columns = [
            lax.dynamic_slice(piece, (0, 0, (s * col_count + col_index) * t), (part, t, t)) for s in range(per_col)
        ]
        mine.append(jnp.stack(columns, 2))
    ordered = []
    for k in range(col_count):
        rows = mine[0]
        for c in range(col_count):
            if c != k:
                rows = jnp.where(col_index == c, mine[c - k] if k < c else mine[col_count - 1 + k - c], rows)
        ordered.append(rows)
    return jnp.concatenate(ordered, 0)


def local(front, child_tiles, tile_owner, tile_slot):
    row_tiles, _, t, col_tiles, _, _ = front.shape
    sub_count = lax.axis_size("sub")
    row_count = lax.axis_size("row")
    col_count = lax.axis_size("col")
    dev_count = sub_count * row_count * col_count
    tile_count = child_tiles.shape[0]
    capacity = max(2, 2 * tile_count // dev_count)
    panel_tiles = NB // t
    per_col = panel_tiles // col_count
    part = row_tiles // col_count
    local_front = front.reshape(row_tiles, t, col_tiles, t)
    sub_index = lax.axis_index("sub")
    row_index = lax.axis_index("row")
    col_index = lax.axis_index("col")
    group_id = sub_index * row_count + row_index

    axes = ("sub", "row", "col")
    indices = (sub_index, row_index, col_index)
    counts = (sub_count, row_count, col_count)
    is_leading = group_id < panel_tiles
    orders = jnp.array([nearest_first(c, col_count) for c in range(col_count)], jnp.int32)
    place = jnp.concatenate(
        [
            jnp.stack([col_index, sub_index, is_leading]).astype(jnp.int32),
            lax.dynamic_index_in_dim(orders, col_index, 0, keepdims=False),
        ]
    )
    where = jnp.stack(
        [jnp.logical_and(is_leading, col_index == 0), jnp.minimum(group_id, panel_tiles - 1)]
        + [col_index ^ i for i in range(col_count)]
    ).astype(jnp.int32)

    def trade(value, axis, index, count):
        value = value.reshape((count, value.shape[0] // count) + value.shape[1:])
        blocks = [lax.dynamic_index_in_dim(value, index, 0, keepdims=False)]
        for i in range(1, count):
            block = lax.dynamic_index_in_dim(value, index ^ i, 0, keepdims=False)
            blocks.append(lax.ppermute(block, axis, [(k, k ^ i) for k in range(count)]))
        return blocks

    def swap(value, axis):
        return lax.all_to_all(value, axis, split_axis=0, concat_axis=0, tiled=True)

    corner = take_corner(local_front, per_col)
    corner, child_tiles = tie(corner, child_tiles)
    corner = lax.all_gather(corner, axes, axis=0)

    cut = capacity // 2
    first, second, targets = pack(
        tile_owner[:, 0], tile_slot, child_tiles, dev_count, cut, capacity - cut, per_col, col_tiles
    )
    targets = jnp.concatenate(
        [targets[:-1].reshape(dev_count, capacity), jnp.broadcast_to(targets[-1], (dev_count, 1))], 1
    )
    targets = swap(targets, axes)
    lost = jnp.sum(targets[:, capacity])
    landing = targets[:, :cut].reshape(-1)
    landing_all = jnp.concatenate([landing, targets[:, cut:capacity].reshape(-1)])
    landing, landing_all, first = tie(landing, landing_all, first)
    arrived = swap(first.reshape(dev_count, cut, t, t), axes).reshape(-1, t, t)
    arrived, second = tie(arrived, second)
    arrived_late = swap(second.reshape(dev_count, capacity - cut, t, t), axes).reshape(-1, t, t)
    panel = assemble_panel(landing, local_front, arrived, per_col)
    corner, panel = tie(corner, panel)
    lower, inverse = factor(corner, panel_tiles, per_col, col_count)

    width = part * sub_count
    row, column = landing_all // col_tiles, landing_all % col_tiles
    area = jnp.where(landing_all < 0, col_count * col_count, (row // part) * col_count + column // width)
    spot = (row % part) * width + column % width

    def update_with(late, up, down, right, so_far, blocks, orders):
        return update(
            area, spot, place, local_front, arrived, late, up, down, right, so_far, blocks, orders, per_col
        )

    def finish(panel, so_far):
        pieces = trade(panel, "col", col_index, col_count)
        solved = solve(where, pieces, inverse, lower).reshape(part, t, NB)
        updated, rows = exchange(solved, arrived_late, update_with, so_far, indices, counts)
        return updated, panel_columns(rows, col_index, col_count, per_col)

    updated, columns = finish(panel, None)

    def again(state):
        _, before, _ = state
        panel = assemble_panel(landing_all, local_front, jnp.concatenate([arrived, arrived_late]), per_col)
        return (jnp.int32(0),) + finish(panel, before)

    _, updated, columns = lax.while_loop(lambda state: state[0] > 0, again, (lost, updated, columns))
    return (updated.reshape(front.shape), columns.reshape(row_tiles, 1, t, per_col, 1, t))


def solution(mesh):
    return jax.shard_map(
        local,
        mesh=mesh,
        in_specs=(
            P(None, ("sub", "row"), None, None, "col", None),
            P(("sub", "row", "col"), None, None),
            P(("sub", "row", "col"), None),
            P(("sub", "row", "col")),
        ),
        out_specs=(
            P(None, ("sub", "row"), None, None, "col", None),
            P(None, ("sub", "row"), None, None, "col", None),
        ),
        check_vma=False,
    )
```

time: 508 us -> 482 us (0.949)
  Pallas kernels: 127 us -> 147 us
  local copies, waits for them, and re-layouts: 42.3 us -> 26.5 us
  waiting for transfers between devices: 207 us -> 195 us
  other arithmetic: 21.9 us -> 13 us
  matrix products: 8.68 us -> 0 us
    all_gather x1, waiting for transfers between devices: 102 us -> 0.02 us  [local(): corner = lax.all_gather(corner, axes, axis=0)]
    all_to_all x2, waiting for transfers between devices: 66.6 us -> 111 us  [swap(): return lax.all_to_all(value, axis, split_axis=0, concat_axis=0, tiled=True)]
    ppermute x6, waiting for transfers between devices: 1.55 us -> 37 us  [along(): return lax.ppermute(value, 'col', pairs)]
    pallas_call x2 -> x6, Pallas kernels: 46.2 us -> 67.8 us  [the longest x3 51.7 us: update(): pl.pallas_call(functools.partial(update_kernel, blocks=tuple(blocks), ord...]
    reshape x9 -> x3, local copies, waits for them, and re-layouts: 20.8 us -> 0.28 us  [the longest x1 0.1 us: local(): landing = targets[:, :cut].reshape(-1)]
    ppermute x16, waiting for transfers between devices: 36.9 us -> 46.2 us  [hop(): return lax.ppermute(value, ('row', 'col'), pairs)]
    dot_general x1 -> x0, matrix products: 8.68 us -> none  [contract(): lax.dot_general(a, b, (((dim_a,), (dim_b,)), ((), ())), precision=EXACT,...]
    dynamic_slice x5 -> x0, local copies, waits for them, and re-layouts: 6.51 us -> none  [local(): lax.dynamic_index_in_dim(piece.reshape(part, t, per_col, col_count, t), c...]
  transfers between devices with their start and end apart: 29 -> 32, of which waited for: 16 -> 15; matrix products, arithmetic and copies ran while one was open for 9% -> 4% of each run, Pallas kernels for 16% -> 26%
where the time goes in v3:
time: 482 us; the launch traced here: 481 us
  waiting for transfers between devices  195 us (40%)
  Pallas kernels  147 us (30%)
  starting transfers between devices  68.7 us (14%)
  local copies, waits for them, and re-layouts  26.5 us (5%)
  between operations  16.1 us (3%)
  blocking collectives  14.2 us (3%)
  other arithmetic  13 us (3%)
    all_to_all x2, waiting for transfers between devices, swap(): return lax.all_to_all(value, axis, split_axis=0, concat_axis=0, tiled=True)  111 us
    pallas_call x1, Pallas kernels, factor(): pl.pallas_call(functools.partial(factor_kernel, tiles=tiles, per_col=per_...  74.4 us
    pallas_call x3, Pallas kernels, update(): pl.pallas_call(functools.partial(update_kernel, blocks=tuple(blocks), ord...  51.7 us
    ppermute x16, waiting for transfers between devices, hop(): return lax.ppermute(value, ('row', 'col'), pairs)  46.2 us
    ppermute x16, starting transfers between devices, hop(): return lax.ppermute(value, ('row', 'col'), pairs)  44.9 us
    ppermute x6, waiting for transfers between devices, along(): return lax.ppermute(value, 'col', pairs)  37 us
    all_to_all x1, blocking collectives, swap(): return lax.all_to_all(value, axis, split_axis=0, concat_axis=0, tiled=True)  14.2 us
  transfers between devices with their start and end apart: 32, of which 15 were waited for; matrix products, arithmetic and copies ran while one was open for 4% of the time, Pallas kernels for 26%

profile of v3, /device:TPU:0, one launch (start us, length us, event | category | flops | bytes accessed | tf_op | source)
XLA Modules:
  0.0 481.0 jit_solution(7063855266890415623)
XLA Ops:
  8.7 6.7 %pack_children.1 = (bf16[128,128,128]{2,1,0:T(8,128)(2,1)}, bf16[128,128,128]{2,1,0:T(8,128)(2,1)}, s32[257]{0:T(512)}) custom-call(s32[128]{0:T(128)} %bitcast.155, s32[128]{0:T(128)} %slot.1, bf16[128,128,128]{2,1,0:T(8,128)(2,1)} %tiles), custom_call_target="tpu_custom_call" | custom-call | bytes 20000000 | tf_op jit(solution)/shard_map/pack_children/pallas_call | solution.py:71
  18.1 14.2 %all_to_all.22 = s32[32,1,9]{2,1,0:T(1,128)S(1)} all-to-all(s32[32,1,9]{2,1,0:T(1,128)S(1)} %bitcast.154), channel_id=1, replica_groups=mesh['sub'=2,'row'=4,'col'=4] {'sub','row','col'}, dimensions={0} | all-to-all | bytes 2304 | tf_op jit(solution)/shard_map/all_to_all | solution.py:691
  33.2 3.6 all-to-all-start.1
  37.6 111.1 %all-to-all-done.1 = bf16[32,4,128,128]{3,2,1,0:T(8,128)(2,1)} async-done(((bf16[32,4,128,128]{3,2,1,0:T(8,128)(2,1)}), bf16[32,4,128,128]{3,2,1,0:T(8,128)(2,1)}, u32[]{:S(2)}, u32[]{:S(2)}) %all-to-all-start.1) | async-done | bytes 4194336 | tf_op jit(solution)/shard_map/all_to_all | solution.py:691
  148.8 4.3 assemble_panel.2
  165.7 74.4 %factor_corner.1 = (bf16[1024,1024]{1,0:T(8,128)(2,1)}, f32[1024,1024]{1,0:T(8,128)S(1)}) custom-call(f32[32,2,128,128]{3,2,1,0:T(8,128)} %bitcast.156), custom_call_target="tpu_custom_call" | custom-call | flops 99999997952 | bytes 200000000 | tf_op jit(solution)/shard_map/factor_corner/pallas_call | solution.py:180
  241.3 7.9 %solve_rows.2 = bf16[512,1024]{1,0:T(8,128)(2,1)} custom-call(s32[6]{0:T(128)S(1)} %stack.170.where, f32[1024,1024]{1,0:T(8,128)S(1)} %get-tuple-element.462.inverse, bf16[1024,1024]{1,0:T(8,128)(2,1)} %get-tuple-element.463.lower, f32[4,2,128,128]{3,2,1,0:T(8,128)} %get-tuple-element.390.rest_0_, f32[4,2,128,128]{3,2,1,0:T(8,128)} %copy-done.56, ...), custom_call_target="tpu_custom_call" | custom-call | flops 8000000000 | bytes 12000000 | tf_op jit(solution)/shard_map/solve_rows/pallas_call | solution.py:325
  259.0 6.5 %collective-permute-done.32 = bf16[2,128,1024]{2,1,0:T(8,128)(2,1)S(1)} collective-permute-done((bf16[2,128,1024]{2,1,0:T(8,128)(2,1)S(1)}, bf16[2,128,1024]{2,1,0:T(8,128)(2,1)S(1)}, u32[]{:S(2)}, u32[]{:S(2)}) %collective-permute-start.32) | collective-permute-done | bytes 524320 | tf_op jit(solution)/shard_map/ppermute | solution.py:573
  265.5 7.1 %collective-permute-done.33 = bf16[2,128,1024]{2,1,0:T(8,128)(2,1)S(1)} collective-permute-done((bf16[2,128,1024]{2,1,0:T(8,128)(2,1)S(1)}, bf16[2,128,1024]{2,1,0:T(8,128)(2,1)S(1)}, u32[]{:S(2)}, u32[]{:S(2)}) %collective-permute-start.33) | collective-permute-done | bytes 524320 | tf_op jit(solution)/shard_map/ppermute | solution.py:573
  276.5 5.3 %collective-permute-start.34 = (bf16[2,128,1024]{2,1,0:T(8,128)(2,1)}, bf16[2,128,1024]{2,1,0:T(8,128)(2,1)}, u32[]{:S(2)}, u32[]{:S(2)}) collective-permute-start(bf16[2,128,1024]{2,1,0:T(8,128)(2,1)} %broadcast_select_fusion.15), channel_id=1, source_target_pairs={{0,8},{4,12},{5,13},{1,9},{10,2},{14,6},{15,7},{11,3},{16,24},{20,... | collective-permute-start | bytes 1572872 | tf_op jit(solution)/shard_map/ppermute | solution.py:573
  281.8 5.7 %collective-permute-done.36.rest_1_ = bf16[4,128,1024]{2,1,0:T(8,128)(2,1)} collective-permute-done((bf16[4,128,1024]{2,1,0:T(8,128)(2,1)}, bf16[4,128,1024]{2,1,0:T(8,128)(2,1)}, u32[]{:S(2)}, u32[]{:S(2)}) %collective-permute-start.36) | collective-permute-done | bytes 1048608 | tf_op jit(solution)/shard_map/ppermute | solution.py:566
  287.5 16.3 %collective-permute-done.37.rest_5_ = bf16[4,128,1024]{2,1,0:T(8,128)(2,1)S(1)} collective-permute-done((bf16[4,128,1024]{2,1,0:T(8,128)(2,1)}, bf16[4,128,1024]{2,1,0:T(8,128)(2,1)S(1)}, u32[]{:S(2)}, u32[]{:S(2)}) %collective-permute-start.37) | collective-permute-done | bytes 1048608 | tf_op jit(solution)/shard_map/ppermute | solution.py:566
  311.5 7.2 %collective-permute-done.38 = bf16[2,128,1024]{2,1,0:T(8,128)(2,1)S(1)} collective-permute-done((bf16[2,128,1024]{2,1,0:T(8,128)(2,1)S(1)}, bf16[2,128,1024]{2,1,0:T(8,128)(2,1)S(1)}, u32[]{:S(2)}, u32[]{:S(2)}) %collective-permute-start.38) | collective-permute-done | bytes 524320 | tf_op jit(solution)/shard_map/ppermute | solution.py:573
  320.4 4.4 collective-permute-start.40
  326.1 8.6 %collective-permute-done.40 = bf16[2,128,1024]{2,1,0:T(8,128)(2,1)S(1)} collective-permute-done((bf16[2,128,1024]{2,1,0:T(8,128)(2,1)S(1)}, bf16[2,128,1024]{2,1,0:T(8,128)(2,1)S(1)}, u32[]{:S(2)}, u32[]{:S(2)}) %collective-permute-start.40) | collective-permute-done | bytes 524320 | tf_op jit(solution)/shard_map/ppermute | solution.py:573
  336.9 14.8 %collective-permute-done.43.rest_6_ = bf16[4,128,1024]{2,1,0:T(8,128)(2,1)S(1)} collective-permute-done((bf16[4,128,1024]{2,1,0:T(8,128)(2,1)S(1)}, bf16[4,128,1024]{2,1,0:T(8,128)(2,1)S(1)}, u32[]{:S(2)}, u32[]{:S(2)}) %collective-permute-start.43) | collective-permute-done | bytes 1048608 | tf_op jit(solution)/shard_map/ppermute | solution.py:566
  354.0 5.7 %collective-permute-start.44 = (bf16[2,128,1024]{2,1,0:T(8,128)(2,1)}, bf16[2,128,1024]{2,1,0:T(8,128)(2,1)}, u32[]{:S(2)}, u32[]{:S(2)}) collective-permute-start(bf16[2,128,1024]{2,1,0:T(8,128)(2,1)} %get-tuple-element.418), channel_id=1, source_target_pairs={{0,4},{5,1},{10,14},{15,11},{16,20},{21,17},{26,30},{31,27}} | collective-permute-start | bytes 1572872 | tf_op jit(solution)/shard_map/ppermute | solution.py:573
  364.7 4.6 collective-permute-done.44
  373.5 4.7 collective-permute-start.46
  381.6 5.8 %collective-permute-done.46 = bf16[2,128,1024]{2,1,0:T(8,128)(2,1)S(1)} collective-permute-done((bf16[2,128,1024]{2,1,0:T(8,128)(2,1)S(1)}, bf16[2,128,1024]{2,1,0:T(8,128)(2,1)S(1)}, u32[]{:S(2)}, u32[]{:S(2)}) %collective-permute-start.46) | collective-permute-done | bytes 524320 | tf_op jit(solution)/shard_map/ppermute | solution.py:573
  390.7 5.4 %collective-permute-start.53 = (bf16[2,128,1024]{2,1,0:T(8,128)(2,1)S(1)}, bf16[2,128,1024]{2,1,0:T(8,128)(2,1)S(1)}, u32[]{:S(2)}, u32[]{:S(2)}) collective-permute-start(bf16[2,128,1024]{2,1,0:T(8,128)(2,1)S(1)} %get-tuple-element.414), channel_id=1, source_target_pairs={{0,4},{5,1},{10,14},{15,11},{16,20},{21,17},{26,30},{31,27}} | collective-permute-start | bytes 1572872 | tf_op jit(solution)/shard_map/ppermute | solution.py:573
  399.5 24.7 %update_blocks.6 = (f32[16,128,32,128]{3,2,1,0:T(8,128)}, s32[8,128]{1,0:T(8,128)}) custom-call(s32[256]{0:T(256)S(1)} %get-tuple-element.464.area, s32[256]{0:T(256)S(1)} %get-tuple-element.465.spot, s32[7]{0:T(128)S(1)} %pad_add_fusion.1.place, s32[32]{0:T(128)} %constant.143.clone.table, f32[16,128,32,128]{3,2,1,0:T(8,128)} %bitcast.112, ...), custom_call_target="tpu_custom_call" | custom-call | flops 8589934592 | bytes 33554432 | tf_op jit(solution)/shard_map/update_blocks/pallas_call | solution.py:506
  431.5 13.4 %update_blocks.7 = (f32[16,128,32,128]{3,2,1,0:T(8,128)}, s32[8,128]{1,0:T(8,128)}) custom-call(s32[256]{0:T(256)S(1)} %get-tuple-element.464.area, s32[256]{0:T(256)S(1)} %get-tuple-element.465.spot, s32[7]{0:T(128)S(1)} %pad_add_fusion.1.place, s32[16]{0:T(128)} %constant.144.clone.table, ...), custom_call_target="tpu_custom_call", output_to_operand_aliasing={{0}: (17, {})} | custom-call | flops 4294967296 | bytes 16777216 | tf_op jit(solution)/shard_map/update_blocks/pallas_call | solution.py:506
  456.5 13.5 %update_blocks.8 = (f32[16,128,32,128]{3,2,1,0:T(8,128)}, s32[8,128]{1,0:T(8,128)}) custom-call(s32[256]{0:T(256)S(1)} %get-tuple-element.464.area, s32[256]{0:T(256)S(1)} %get-tuple-element.465.spot, s32[7]{0:T(128)S(1)} %pad_add_fusion.1.place, s32[16]{0:T(128)} %constant.145.clone.table, ...), custom_call_target="tpu_custom_call", output_to_operand_aliasing={{0}: (17, {})} | custom-call | flops 4294967296 | bytes 16777216 | tf_op jit(solution)/shard_map/update_blocks/pallas_call | solution.py:506
  (161 shorter events, 88.6 us)
Async XLA Ops:
  33.2 115.6 %all-to-all-start.1 = ((bf16[32,4,128,128]{3,2,1,0:T(8,128)(2,1)}), bf16[32,4,128,128]{3,2,1,0:T(8,128)(2,1)}, u32[]{:S(2)}, u32[]{:S(2)}) async-start(bf16[32,4,128,128]{3,2,1,0:T(8,128)(2,1)} %bitcast.150), calls=%async_computation.1 | async-start | bytes 8388608 | tf_op jit(solution)/shard_map/all_to_all | solution.py:691
  36.8 116.3 %all-gather.3.cloned.1.call-start = ((), (), s32[]{:S(2)}) async-start(), calls=%async_computation.3 | async-start | bytes 4325376 | tf_op jit(solution)/shard_map/all_gather | solution.py:695
  155.7 84.5 %collective-permute-start.29 = (f32[4,2,128,128]{3,2,1,0:T(8,128)S(1)}, f32[4,2,128,128]{3,2,1,0:T(8,128)S(1)}, u32[]{:S(2)}, u32[]{:S(2)}) collective-permute-start(f32[4,2,128,128]{3,2,1,0:T(8,128)S(1)} %get-tuple-element.389), channel_id=1, source_target_pairs={{0,1},{1,0},{2,3},{3,2},{4,5},{5,4},{6,7},{7,6},{8,9},{9,8},{10,11... | collective-permute-start | bytes 1572872 | tf_op jit(solution)/shard_map/ppermute | solution.py:687
  158.6 81.6 %collective-permute-start.30 = (f32[4,2,128,128]{3,2,1,0:T(8,128)S(1)}, f32[4,2,128,128]{3,2,1,0:T(8,128)S(1)}, u32[]{:S(2)}, u32[]{:S(2)}) collective-permute-start(f32[4,2,128,128]{3,2,1,0:T(8,128)S(1)} %get-tuple-element.388), channel_id=1, source_target_pairs={{0,2},{1,3},{2,0},{3,1},{4,6},{5,7},{6,4},{7,5},{8,10},{9,11},{10,... | collective-permute-start | bytes 1572872 | tf_op jit(solution)/shard_map/ppermute | solution.py:687
  160.6 79.5 %collective-permute-start.31 = (f32[4,2,128,128]{3,2,1,0:T(8,128)S(1)}, f32[4,2,128,128]{3,2,1,0:T(8,128)S(1)}, u32[]{:S(2)}, u32[]{:S(2)}) collective-permute-start(f32[4,2,128,128]{3,2,1,0:T(8,128)S(1)} %get-tuple-element.387), channel_id=1, source_target_pairs={{0,3},{1,2},{2,1},{3,0},{4,7},{5,6},{6,5},{7,4},{8,11},{9,10},{10,... | collective-permute-start | bytes 1572872 | tf_op jit(solution)/shard_map/ppermute | solution.py:687
  162.1 141.8 %all-to-all-start.2 = ((bf16[32,4,128,128]{3,2,1,0:T(8,128)(2,1)}), bf16[32,4,128,128]{3,2,1,0:T(8,128)(2,1)}, u32[]{:S(2)}, u32[]{:S(2)}) async-start(bf16[32,4,128,128]{3,2,1,0:T(8,128)(2,1)} %bitcast.149), calls=%async_computation.2 | async-start | bytes 8388608 | tf_op jit(solution)/shard_map/all_to_all | solution.py:691
  250.5 14.9 %collective-permute-start.32 = (bf16[2,128,1024]{2,1,0:T(8,128)(2,1)S(1)}, bf16[2,128,1024]{2,1,0:T(8,128)(2,1)S(1)}, u32[]{:S(2)}, u32[]{:S(2)}) collective-permute-start(bf16[2,128,1024]{2,1,0:T(8,128)(2,1)S(1)} %bitcast.146), channel_id=1, source_target_pairs={{0,4},{5,1},{10,14},{15,11},{16,20},{21,17},{26,30},{31,27}} | collective-permute-start | bytes 1572872 | tf_op jit(solution)/shard_map/ppermute | solution.py:573
  254.0 18.5 %collective-permute-start.33 = (bf16[2,128,1024]{2,1,0:T(8,128)(2,1)S(1)}, bf16[2,128,1024]{2,1,0:T(8,128)(2,1)S(1)}, u32[]{:S(2)}, u32[]{:S(2)}) collective-permute-start(bf16[2,128,1024]{2,1,0:T(8,128)(2,1)S(1)} %bitcast.143), channel_id=1, source_target_pairs={{0,8},{5,13},{10,2},{15,7},{16,24},{21,29},{26,18},{31,23}} | collective-permute-start | bytes 1572872 | tf_op jit(solution)/shard_map/ppermute | solution.py:573
  255.4 32.1 %collective-permute-start.36 = (bf16[4,128,1024]{2,1,0:T(8,128)(2,1)}, bf16[4,128,1024]{2,1,0:T(8,128)(2,1)}, u32[]{:S(2)}, u32[]{:S(2)}) collective-permute-start(bf16[4,128,1024]{2,1,0:T(8,128)(2,1)} %bitcast.133), channel_id=1, source_target_pairs={{0,1},{1,2},{2,3},{4,5},{5,6},{6,7},{8,9},{9,10},{10,11},{12,13},{... | collective-permute-start | bytes 3145736 | tf_op jit(solution)/shard_map/ppermute | solution.py:566
  257.7 46.2 %collective-permute-start.37 = (bf16[4,128,1024]{2,1,0:T(8,128)(2,1)}, bf16[4,128,1024]{2,1,0:T(8,128)(2,1)S(1)}, u32[]{:S(2)}, u32[]{:S(2)}) collective-permute-start(bf16[4,128,1024]{2,1,0:T(8,128)(2,1)} %bitcast.134), channel_id=1, source_target_pairs={{1,0},{2,1},{3,2},{5,4},{6,5},{7,6},{9,8},{10,9},{11,10},{13,12},{... | collective-permute-start | bytes 3145736 | tf_op jit(solution)/shard_map/ppermute | solution.py:566
  273.5 30.3 %collective-permute-start.35 = (bf16[2,128,1024]{2,1,0:T(8,128)(2,1)}, bf16[2,128,1024]{2,1,0:T(8,128)(2,1)}, u32[]{:S(2)}, u32[]{:S(2)}) collective-permute-start(bf16[2,128,1024]{2,1,0:T(8,128)(2,1)} %broadcast_select_fusion.14), channel_id=1, source_target_pairs={{0,4},{8,12},{5,1},{13,9},{10,14},{2,6},{15,11},{7,3},{16,20},{24,... | collective-permute-start | bytes 1572872 | tf_op jit(solution)/shard_map/ppermute | solution.py:573
  276.5 27.4 %collective-permute-start.34 = (bf16[2,128,1024]{2,1,0:T(8,128)(2,1)}, bf16[2,128,1024]{2,1,0:T(8,128)(2,1)}, u32[]{:S(2)}, u32[]{:S(2)}) collective-permute-start(bf16[2,128,1024]{2,1,0:T(8,128)(2,1)} %broadcast_select_fusion.15), channel_id=1, source_target_pairs={{0,8},{4,12},{5,13},{1,9},{10,2},{14,6},{15,7},{11,3},{16,24},{20,... | collective-permute-start | bytes 1572872 | tf_op jit(solution)/shard_map/ppermute | solution.py:573
  309.4 26.7 %collective-permute-start.42 = (bf16[4,128,1024]{2,1,0:T(8,128)(2,1)}, bf16[4,128,1024]{2,1,0:T(8,128)(2,1)S(1)}, u32[]{:S(2)}, u32[]{:S(2)}) collective-permute-start(bf16[4,128,1024]{2,1,0:T(8,128)(2,1)} %collective-permute-done.36.rest_1_), channel_id=1, source_target_pairs={{1,2},{2,3},{5,6},{6,7},{9,10},{10,11},{13,14},{14,15},{17,18},{18... | collective-permute-start | bytes 3145736 | tf_op jit(solution)/shard_map/ppermute | solution.py:566
  310.2 41.5 %collective-permute-start.43 = (bf16[4,128,1024]{2,1,0:T(8,128)(2,1)S(1)}, bf16[4,128,1024]{2,1,0:T(8,128)(2,1)S(1)}, u32[]{:S(2)}, u32[]{:S(2)}) collective-permute-start(bf16[4,128,1024]{2,1,0:T(8,128)(2,1)S(1)} %collective-permute-done.37.rest_5_), channel_id=1, source_target_pairs={{1,0},{2,1},{5,4},{6,5},{9,8},{10,9},{13,12},{14,13},{17,16},{18,1... | collective-permute-start | bytes 3145736 | tf_op jit(solution)/shard_map/ppermute | solution.py:566
  320.4 14.4 %collective-permute-start.40 = (bf16[2,128,1024]{2,1,0:T(8,128)(2,1)S(1)}, bf16[2,128,1024]{2,1,0:T(8,128)(2,1)S(1)}, u32[]{:S(2)}, u32[]{:S(2)}) collective-permute-start(bf16[2,128,1024]{2,1,0:T(8,128)(2,1)S(1)} %get-tuple-element.420), channel_id=1, source_target_pairs={{0,8},{4,12},{5,13},{1,9},{10,2},{14,6},{15,7},{11,3},{16,24},{20,... | collective-permute-start | bytes 1572872 | tf_op jit(solution)/shard_map/ppermute | solution.py:573
  354.0 15.3 %collective-permute-start.44 = (bf16[2,128,1024]{2,1,0:T(8,128)(2,1)}, bf16[2,128,1024]{2,1,0:T(8,128)(2,1)}, u32[]{:S(2)}, u32[]{:S(2)}) collective-permute-start(bf16[2,128,1024]{2,1,0:T(8,128)(2,1)} %get-tuple-element.418), channel_id=1, source_target_pairs={{0,4},{5,1},{10,14},{15,11},{16,20},{21,17},{26,30},{31,27}} | collective-permute-start | bytes 1572872 | tf_op jit(solution)/shard_map/ppermute | solution.py:573
  362.7 26.0 %collective-permute-start.48 = (bf16[4,128,1024]{2,1,0:T(8,128)(2,1)S(1)}, bf16[4,128,1024]{2,1,0:T(8,128)(2,1)S(1)}, u32[]{:S(2)}, u32[]{:S(2)}) collective-permute-start(bf16[4,128,1024]{2,1,0:T(8,128)(2,1)S(1)} %collective-permute-done.42.rest_2_), channel_id=1, source_target_pairs={{2,3},{6,7},{10,11},{14,15},{18,19},{22,23},{26,27},{30,31}} | collective-permute-start | bytes 3145736 | tf_op jit(solution)/shard_map/ppermute | solution.py:566
  363.4 25.4 %collective-permute-start.49 = (bf16[4,128,1024]{2,1,0:T(8,128)(2,1)S(1)}, bf16[4,128,1024]{2,1,0:T(8,128)(2,1)S(1)}, u32[]{:S(2)}, u32[]{:S(2)}) collective-permute-start(bf16[4,128,1024]{2,1,0:T(8,128)(2,1)S(1)} %collective-permute-done.43.rest_6_), channel_id=1, source_target_pairs={{1,0},{5,4},{9,8},{13,12},{17,16},{21,20},{25,24},{29,28}} | collective-permute-start | bytes 3145736 | tf_op jit(solution)/shard_map/ppermute | solution.py:566
  381.5 16.0 %collective-permute-start.50 = (bf16[4,128,1024]{2,1,0:T(8,128)(2,1)S(1)}, bf16[4,128,1024]{2,1,0:T(8,128)(2,1)S(1)}, u32[]{:S(2)}, u32[]{:S(2)}) collective-permute-start(bf16[4,128,1024]{2,1,0:T(8,128)(2,1)S(1)} %pad_maximum_fusion.11.rest_8_), channel_id=1, source_target_pairs={{0,16},{16,0},{1,17},{17,1},{2,18},{18,2},{3,19},{19,3},{4,20},{20... | collective-permute-start | bytes 3145736 | tf_op jit(solution)/shard_map/ppermute | solution.py:624
  390.4 41.1 %collective-permute-start.52 = (bf16[4,128,1024]{2,1,0:T(8,128)(2,1)}, bf16[4,128,1024]{2,1,0:T(8,128)(2,1)}, u32[]{:S(2)}, u32[]{:S(2)}) collective-permute-start(bf16[4,128,1024]{2,1,0:T(8,128)(2,1)} %pad_maximum_fusion.13.rest_8_), channel_id=1, source_target_pairs={{0,16},{16,0},{1,17},{17,1},{2,18},{18,2},{3,19},{19,3},{4,20},{20... | collective-permute-start | bytes 3145736 | tf_op jit(solution)/shard_map/ppermute | solution.py:624
  390.7 35.4 %collective-permute-start.53 = (bf16[2,128,1024]{2,1,0:T(8,128)(2,1)S(1)}, bf16[2,128,1024]{2,1,0:T(8,128)(2,1)S(1)}, u32[]{:S(2)}, u32[]{:S(2)}) collective-permute-start(bf16[2,128,1024]{2,1,0:T(8,128)(2,1)S(1)} %get-tuple-element.414), channel_id=1, source_target_pairs={{0,4},{5,1},{10,14},{15,11},{16,20},{21,17},{26,30},{31,27}} | collective-permute-start | bytes 1572872 | tf_op jit(solution)/shard_map/ppermute | solution.py:573
  396.1 30.0 %collective-permute-start.54 = (bf16[2,128,1024]{2,1,0:T(8,128)(2,1)S(1)}, bf16[2,128,1024]{2,1,0:T(8,128)(2,1)S(1)}, u32[]{:S(2)}, u32[]{:S(2)}) collective-permute-start(bf16[2,128,1024]{2,1,0:T(8,128)(2,1)S(1)} %get-tuple-element.413), channel_id=1, source_target_pairs={{0,8},{5,13},{10,2},{15,7},{16,24},{21,29},{26,18},{31,23}} | collective-permute-start | bytes 1572872 | tf_op jit(solution)/shard_map/ppermute | solution.py:573
  427.2 19.7 %collective-permute-start.55 = (bf16[2,128,1024]{2,1,0:T(8,128)(2,1)}, bf16[2,128,1024]{2,1,0:T(8,128)(2,1)S(1)}, u32[]{:S(2)}, u32[]{:S(2)}) collective-permute-start(bf16[2,128,1024]{2,1,0:T(8,128)(2,1)} %get-tuple-element.410), channel_id=1, source_target_pairs={{0,8},{4,12},{5,13},{1,9},{10,2},{14,6},{15,7},{11,3},{16,24},{20,... | collective-permute-start | bytes 1572872 | tf_op jit(solution)/shard_map/ppermute | solution.py:573
  428.5 18.4 %collective-permute-start.56 = (bf16[2,128,1024]{2,1,0:T(8,128)(2,1)}, bf16[2,128,1024]{2,1,0:T(8,128)(2,1)S(1)}, u32[]{:S(2)}, u32[]{:S(2)}) collective-permute-start(bf16[2,128,1024]{2,1,0:T(8,128)(2,1)} %get-tuple-element.409), channel_id=1, source_target_pairs={{0,4},{8,12},{5,1},{13,9},{10,14},{2,6},{15,11},{7,3},{16,20},{24,... | collective-permute-start | bytes 1572872 | tf_op jit(solution)/shard_map/ppermute | solution.py:573
  (40 other events, 1002.5 us)
Sparse Core Ops, SparseCore 0:
  41.2 95.4 all-gather.2

commit v4 on v3

--- a/solution.py
+++ b/solution.py
@@ -396,7 +396,8 @@
                 pltpu.make_async_copy(
                     right[n * sub_count + i].at[r], right_v.at[n, r * sub_count + origin], right_sem
                 ).start()
-    for b in range(min(depth - 1, steps)):
+    ahead = depth - 2
+    for b in range(min(ahead, steps)):
         read(b, b)
 
     for k in range(count * count + 1):
@@ -450,15 +451,15 @@
     def step(b, _):
         slot = lax.rem(b, depth)
 
-        @pl.when(b + depth - 1 < steps)
+        @pl.when(b + ahead < steps)
         def _():
-            later = lax.rem(b + depth - 1, depth)
-
-            @pl.when(b >= 1)
+            later = lax.rem(b + ahead, depth)
+
+            @pl.when(b + ahead >= depth)
             def _():
                 drain(later, out_sem)
 
-            read(b + depth - 1, later)
+            read(b + ahead, later)
 
         drain(slot, in_sem)
         rows = left_v[table[4 * b + 2]].reshape(part * t, left_v.shape[-1])
@@ -490,7 +491,7 @@
     count = len(orders)
     row_used = sorted({i for i, _ in blocks})
     col_used = sorted({j for _, j in blocks})
-    depth = min(4, len(blocks))
+    depth = max(3, min(5, len(blocks) + 1))
     reach = len(up)
     any_spec = pl.BlockSpec(memory_space=ANY)
     smem = pl.BlockSpec(memory_space=pltpu.SMEM)

time: 482 us -> 476 us (0.988)
  no operation moved by 1% of the time
where the time goes in v4:
time: 476 us; the launch traced here: 475 us
  waiting for transfers between devices  193 us (41%)
  Pallas kernels  144 us (30%)
  starting transfers between devices  66.8 us (14%)
  local copies, waits for them, and re-layouts  26.8 us (6%)
  between operations  16.1 us (3%)
  blocking collectives  14.2 us (3%)
  other arithmetic  12.8 us (3%)
    all_to_all x2, waiting for transfers between devices, swap(): return lax.all_to_all(value, axis, split_axis=0, concat_axis=0, tiled=True)  111 us
    pallas_call x1, Pallas kernels, factor(): pl.pallas_call(functools.partial(factor_kernel, tiles=tiles, per_col=per_...  74.4 us
    pallas_call x3, Pallas kernels, update(): pl.pallas_call(functools.partial(update_kernel, blocks=tuple(blocks), ord...  49.4 us
    ppermute x16, starting transfers between devices, hop(): return lax.ppermute(value, ('row', 'col'), pairs)  45.3 us
    ppermute x16, waiting for transfers between devices, hop(): return lax.ppermute(value, ('row', 'col'), pairs)  44.9 us
    ppermute x6, waiting for transfers between devices, along(): return lax.ppermute(value, 'col', pairs)  36.4 us
    all_to_all x1, blocking collectives, swap(): return lax.all_to_all(value, axis, split_axis=0, concat_axis=0, tiled=True)  14.2 us
  transfers between devices with their start and end apart: 32, of which 15 were waited for; matrix products, arithmetic and copies ran while one was open for 4% of the time, Pallas kernels for 26%

profile of v4, /device:TPU:0, one launch (start us, length us, event | category | flops | bytes accessed | tf_op | source)
XLA Modules:
  0.0 475.0 jit_solution(17083329085120615439)
XLA Ops:
  8.7 6.7 %pack_children.1 = (bf16[128,128,128]{2,1,0:T(8,128)(2,1)}, bf16[128,128,128]{2,1,0:T(8,128)(2,1)}, s32[257]{0:T(512)}) custom-call(s32[128]{0:T(128)} %bitcast.155, s32[128]{0:T(128)} %slot.1, bf16[128,128,128]{2,1,0:T(8,128)(2,1)} %tiles), custom_call_target="tpu_custom_call" | custom-call | bytes 20000000 | tf_op jit(solution)/shard_map/pack_children/pallas_call | solution.py:71
  18.1 14.2 %all_to_all.22 = s32[32,1,9]{2,1,0:T(1,128)S(1)} all-to-all(s32[32,1,9]{2,1,0:T(1,128)S(1)} %bitcast.154), channel_id=1, replica_groups=mesh['sub'=2,'row'=4,'col'=4] {'sub','row','col'}, dimensions={0} | all-to-all | bytes 2304 | tf_op jit(solution)/shard_map/all_to_all | solution.py:692
  33.2 3.6 all-to-all-start.1
  37.6 111.1 %all-to-all-done.1 = bf16[32,4,128,128]{3,2,1,0:T(8,128)(2,1)} async-done(((bf16[32,4,128,128]{3,2,1,0:T(8,128)(2,1)}), bf16[32,4,128,128]{3,2,1,0:T(8,128)(2,1)}, u32[]{:S(2)}, u32[]{:S(2)}) %all-to-all-start.1) | async-done | bytes 4194336 | tf_op jit(solution)/shard_map/all_to_all | solution.py:692
  148.8 4.3 assemble_panel.2
  165.7 74.4 %factor_corner.1 = (bf16[1024,1024]{1,0:T(8,128)(2,1)}, f32[1024,1024]{1,0:T(8,128)S(1)}) custom-call(f32[32,2,128,128]{3,2,1,0:T(8,128)} %bitcast.156), custom_call_target="tpu_custom_call" | custom-call | flops 99999997952 | bytes 200000000 | tf_op jit(solution)/shard_map/factor_corner/pallas_call | solution.py:180
  241.3 7.9 %solve_rows.2 = bf16[512,1024]{1,0:T(8,128)(2,1)} custom-call(s32[6]{0:T(128)S(1)} %stack.170.where, f32[1024,1024]{1,0:T(8,128)S(1)} %get-tuple-element.462.inverse, bf16[1024,1024]{1,0:T(8,128)(2,1)} %get-tuple-element.463.lower, f32[4,2,128,128]{3,2,1,0:T(8,128)} %get-tuple-element.390.rest_0_, f32[4,2,128,128]{3,2,1,0:T(8,128)} %copy-done.56, ...), custom_call_target="tpu_custom_call" | custom-call | flops 8000000000 | bytes 12000000 | tf_op jit(solution)/shard_map/solve_rows/pallas_call | solution.py:325
  259.0 6.5 %collective-permute-done.32 = bf16[2,128,1024]{2,1,0:T(8,128)(2,1)S(1)} collective-permute-done((bf16[2,128,1024]{2,1,0:T(8,128)(2,1)S(1)}, bf16[2,128,1024]{2,1,0:T(8,128)(2,1)S(1)}, u32[]{:S(2)}, u32[]{:S(2)}) %collective-permute-start.32) | collective-permute-done | bytes 524320 | tf_op jit(solution)/shard_map/ppermute | solution.py:574
  265.5 7.0 %collective-permute-done.33 = bf16[2,128,1024]{2,1,0:T(8,128)(2,1)S(1)} collective-permute-done((bf16[2,128,1024]{2,1,0:T(8,128)(2,1)S(1)}, bf16[2,128,1024]{2,1,0:T(8,128)(2,1)S(1)}, u32[]{:S(2)}, u32[]{:S(2)}) %collective-permute-start.33) | collective-permute-done | bytes 524320 | tf_op jit(solution)/shard_map/ppermute | solution.py:574
  276.5 5.3 %collective-permute-start.34 = (bf16[2,128,1024]{2,1,0:T(8,128)(2,1)}, bf16[2,128,1024]{2,1,0:T(8,128)(2,1)}, u32[]{:S(2)}, u32[]{:S(2)}) collective-permute-start(bf16[2,128,1024]{2,1,0:T(8,128)(2,1)} %broadcast_select_fusion.15), channel_id=1, source_target_pairs={{0,8},{4,12},{5,13},{1,9},{10,2},{14,6},{15,7},{11,3},{16,24},{20,... | collective-permute-start | bytes 1572872 | tf_op jit(solution)/shard_map/ppermute | solution.py:574
  281.8 3.6 collective-permute-done.36.rest_1_
  285.4 17.8 %collective-permute-done.37.rest_5_ = bf16[4,128,1024]{2,1,0:T(8,128)(2,1)S(1)} collective-permute-done((bf16[4,128,1024]{2,1,0:T(8,128)(2,1)}, bf16[4,128,1024]{2,1,0:T(8,128)(2,1)S(1)}, u32[]{:S(2)}, u32[]{:S(2)}) %collective-permute-start.37) | collective-permute-done | bytes 1048608 | tf_op jit(solution)/shard_map/ppermute | solution.py:567
  311.6 7.3 %collective-permute-done.38 = bf16[2,128,1024]{2,1,0:T(8,128)(2,1)S(1)} collective-permute-done((bf16[2,128,1024]{2,1,0:T(8,128)(2,1)S(1)}, bf16[2,128,1024]{2,1,0:T(8,128)(2,1)S(1)}, u32[]{:S(2)}, u32[]{:S(2)}) %collective-permute-start.38) | collective-permute-done | bytes 524320 | tf_op jit(solution)/shard_map/ppermute | solution.py:574
  320.3 4.4 collective-permute-start.40
  326.1 8.5 %collective-permute-done.40 = bf16[2,128,1024]{2,1,0:T(8,128)(2,1)S(1)} collective-permute-done((bf16[2,128,1024]{2,1,0:T(8,128)(2,1)S(1)}, bf16[2,128,1024]{2,1,0:T(8,128)(2,1)S(1)}, u32[]{:S(2)}, u32[]{:S(2)}) %collective-permute-start.40) | collective-permute-done | bytes 524320 | tf_op jit(solution)/shard_map/ppermute | solution.py:574
  336.7 14.4 %collective-permute-done.43.rest_6_ = bf16[4,128,1024]{2,1,0:T(8,128)(2,1)S(1)} collective-permute-done((bf16[4,128,1024]{2,1,0:T(8,128)(2,1)S(1)}, bf16[4,128,1024]{2,1,0:T(8,128)(2,1)S(1)}, u32[]{:S(2)}, u32[]{:S(2)}) %collective-permute-start.43) | collective-permute-done | bytes 1048608 | tf_op jit(solution)/shard_map/ppermute | solution.py:567
  353.4 5.2 %collective-permute-start.44 = (bf16[2,128,1024]{2,1,0:T(8,128)(2,1)}, bf16[2,128,1024]{2,1,0:T(8,128)(2,1)}, u32[]{:S(2)}, u32[]{:S(2)}) collective-permute-start(bf16[2,128,1024]{2,1,0:T(8,128)(2,1)} %get-tuple-element.418), channel_id=1, source_target_pairs={{0,4},{5,1},{10,14},{15,11},{16,20},{21,17},{26,30},{31,27}} | collective-permute-start | bytes 1572872 | tf_op jit(solution)/shard_map/ppermute | solution.py:574
  364.1 3.7 collective-permute-done.44
  372.4 4.7 collective-permute-start.46
  380.4 5.4 %collective-permute-done.46 = bf16[2,128,1024]{2,1,0:T(8,128)(2,1)S(1)} collective-permute-done((bf16[2,128,1024]{2,1,0:T(8,128)(2,1)S(1)}, bf16[2,128,1024]{2,1,0:T(8,128)(2,1)S(1)}, u32[]{:S(2)}, u32[]{:S(2)}) %collective-permute-start.46) | collective-permute-done | bytes 524320 | tf_op jit(solution)/shard_map/ppermute | solution.py:574
  389.3 5.2 %collective-permute-start.53 = (bf16[2,128,1024]{2,1,0:T(8,128)(2,1)S(1)}, bf16[2,128,1024]{2,1,0:T(8,128)(2,1)S(1)}, u32[]{:S(2)}, u32[]{:S(2)}) collective-permute-start(bf16[2,128,1024]{2,1,0:T(8,128)(2,1)S(1)} %get-tuple-element.414), channel_id=1, source_target_pairs={{0,4},{5,1},{10,14},{15,11},{16,20},{21,17},{26,30},{31,27}} | collective-permute-start | bytes 1572872 | tf_op jit(solution)/shard_map/ppermute | solution.py:574
  397.8 20.8 %update_blocks.6 = (f32[16,128,32,128]{3,2,1,0:T(8,128)}, s32[8,128]{1,0:T(8,128)}) custom-call(s32[256]{0:T(256)S(1)} %get-tuple-element.464.area, s32[256]{0:T(256)S(1)} %get-tuple-element.465.spot, s32[7]{0:T(128)S(1)} %pad_add_fusion.1.place, s32[32]{0:T(128)} %constant.143.clone.table, f32[16,128,32,128]{3,2,1,0:T(8,128)} %bitcast.112, ...), custom_call_target="tpu_custom_call" | custom-call | flops 8589934592 | bytes 33554432 | tf_op jit(solution)/shard_map/update_blocks/pallas_call | solution.py:507
  426.0 14.4 %update_blocks.7 = (f32[16,128,32,128]{3,2,1,0:T(8,128)}, s32[8,128]{1,0:T(8,128)}) custom-call(s32[256]{0:T(256)S(1)} %get-tuple-element.464.area, s32[256]{0:T(256)S(1)} %get-tuple-element.465.spot, s32[7]{0:T(128)S(1)} %pad_add_fusion.1.place, s32[16]{0:T(128)} %constant.144.clone.table, ...), custom_call_target="tpu_custom_call", output_to_operand_aliasing={{0}: (17, {})} | custom-call | flops 4294967296 | bytes 16777216 | tf_op jit(solution)/shard_map/update_blocks/pallas_call | solution.py:507
  449.8 14.2 %update_blocks.8 = (f32[16,128,32,128]{3,2,1,0:T(8,128)}, s32[8,128]{1,0:T(8,128)}) custom-call(s32[256]{0:T(256)S(1)} %get-tuple-element.464.area, s32[256]{0:T(256)S(1)} %get-tuple-element.465.spot, s32[7]{0:T(128)S(1)} %pad_add_fusion.1.place, s32[16]{0:T(128)} %constant.145.clone.table, ...), custom_call_target="tpu_custom_call", output_to_operand_aliasing={{0}: (17, {})} | custom-call | flops 4294967296 | bytes 16777216 | tf_op jit(solution)/shard_map/update_blocks/pallas_call | solution.py:507
  (161 shorter events, 88.1 us)
Async XLA Ops:
  33.2 115.6 %all-to-all-start.1 = ((bf16[32,4,128,128]{3,2,1,0:T(8,128)(2,1)}), bf16[32,4,128,128]{3,2,1,0:T(8,128)(2,1)}, u32[]{:S(2)}, u32[]{:S(2)}) async-start(bf16[32,4,128,128]{3,2,1,0:T(8,128)(2,1)} %bitcast.150), calls=%async_computation.1 | async-start | bytes 8388608 | tf_op jit(solution)/shard_map/all_to_all | solution.py:692
  36.8 116.3 %all-gather.3.cloned.1.call-start = ((), (), s32[]{:S(2)}) async-start(), calls=%async_computation.3 | async-start | bytes 4325376 | tf_op jit(solution)/shard_map/all_gather | solution.py:696
  155.6 84.5 %collective-permute-start.29 = (f32[4,2,128,128]{3,2,1,0:T(8,128)S(1)}, f32[4,2,128,128]{3,2,1,0:T(8,128)S(1)}, u32[]{:S(2)}, u32[]{:S(2)}) collective-permute-start(f32[4,2,128,128]{3,2,1,0:T(8,128)S(1)} %get-tuple-element.389), channel_id=1, source_target_pairs={{0,1},{1,0},{2,3},{3,2},{4,5},{5,4},{6,7},{7,6},{8,9},{9,8},{10,11... | collective-permute-start | bytes 1572872 | tf_op jit(solution)/shard_map/ppermute | solution.py:688
  159.0 81.2 %collective-permute-start.30 = (f32[4,2,128,128]{3,2,1,0:T(8,128)S(1)}, f32[4,2,128,128]{3,2,1,0:T(8,128)S(1)}, u32[]{:S(2)}, u32[]{:S(2)}) collective-permute-start(f32[4,2,128,128]{3,2,1,0:T(8,128)S(1)} %get-tuple-element.388), channel_id=1, source_target_pairs={{0,2},{1,3},{2,0},{3,1},{4,6},{5,7},{6,4},{7,5},{8,10},{9,11},{10,... | collective-permute-start | bytes 1572872 | tf_op jit(solution)/shard_map/ppermute | solution.py:688
  160.7 79.5 %collective-permute-start.31 = (f32[4,2,128,128]{3,2,1,0:T(8,128)S(1)}, f32[4,2,128,128]{3,2,1,0:T(8,128)S(1)}, u32[]{:S(2)}, u32[]{:S(2)}) collective-permute-start(f32[4,2,128,128]{3,2,1,0:T(8,128)S(1)} %get-tuple-element.387), channel_id=1, source_target_pairs={{0,3},{1,2},{2,1},{3,0},{4,7},{5,6},{6,5},{7,4},{8,11},{9,10},{10,... | collective-permute-start | bytes 1572872 | tf_op jit(solution)/shard_map/ppermute | solution.py:688
  162.1 141.1 %all-to-all-start.2 = ((bf16[32,4,128,128]{3,2,1,0:T(8,128)(2,1)}), bf16[32,4,128,128]{3,2,1,0:T(8,128)(2,1)}, u32[]{:S(2)}, u32[]{:S(2)}) async-start(bf16[32,4,128,128]{3,2,1,0:T(8,128)(2,1)} %bitcast.149), calls=%async_computation.2 | async-start | bytes 8388608 | tf_op jit(solution)/shard_map/all_to_all | solution.py:692
  250.6 15.0 %collective-permute-start.32 = (bf16[2,128,1024]{2,1,0:T(8,128)(2,1)S(1)}, bf16[2,128,1024]{2,1,0:T(8,128)(2,1)S(1)}, u32[]{:S(2)}, u32[]{:S(2)}) collective-permute-start(bf16[2,128,1024]{2,1,0:T(8,128)(2,1)S(1)} %bitcast.146), channel_id=1, source_target_pairs={{0,4},{5,1},{10,14},{15,11},{16,20},{21,17},{26,30},{31,27}} | collective-permute-start | bytes 1572872 | tf_op jit(solution)/shard_map/ppermute | solution.py:574
  254.1 18.5 %collective-permute-start.33 = (bf16[2,128,1024]{2,1,0:T(8,128)(2,1)S(1)}, bf16[2,128,1024]{2,1,0:T(8,128)(2,1)S(1)}, u32[]{:S(2)}, u32[]{:S(2)}) collective-permute-start(bf16[2,128,1024]{2,1,0:T(8,128)(2,1)S(1)} %bitcast.143), channel_id=1, source_target_pairs={{0,8},{5,13},{10,2},{15,7},{16,24},{21,29},{26,18},{31,23}} | collective-permute-start | bytes 1572872 | tf_op jit(solution)/shard_map/ppermute | solution.py:574
  255.4 30.0 %collective-permute-start.36 = (bf16[4,128,1024]{2,1,0:T(8,128)(2,1)}, bf16[4,128,1024]{2,1,0:T(8,128)(2,1)}, u32[]{:S(2)}, u32[]{:S(2)}) collective-permute-start(bf16[4,128,1024]{2,1,0:T(8,128)(2,1)} %bitcast.133), channel_id=1, source_target_pairs={{0,1},{1,2},{2,3},{4,5},{5,6},{6,7},{8,9},{9,10},{10,11},{12,13},{... | collective-permute-start | bytes 3145736 | tf_op jit(solution)/shard_map/ppermute | solution.py:567
  257.7 45.5 %collective-permute-start.37 = (bf16[4,128,1024]{2,1,0:T(8,128)(2,1)}, bf16[4,128,1024]{2,1,0:T(8,128)(2,1)S(1)}, u32[]{:S(2)}, u32[]{:S(2)}) collective-permute-start(bf16[4,128,1024]{2,1,0:T(8,128)(2,1)} %bitcast.134), channel_id=1, source_target_pairs={{1,0},{2,1},{3,2},{5,4},{6,5},{7,6},{9,8},{10,9},{11,10},{13,12},{... | collective-permute-start | bytes 3145736 | tf_op jit(solution)/shard_map/ppermute | solution.py:567
  273.5 29.8 %collective-permute-start.35 = (bf16[2,128,1024]{2,1,0:T(8,128)(2,1)}, bf16[2,128,1024]{2,1,0:T(8,128)(2,1)}, u32[]{:S(2)}, u32[]{:S(2)}) collective-permute-start(bf16[2,128,1024]{2,1,0:T(8,128)(2,1)} %broadcast_select_fusion.14), channel_id=1, source_target_pairs={{0,4},{8,12},{5,1},{13,9},{10,14},{2,6},{15,11},{7,3},{16,20},{24,... | collective-permute-start | bytes 1572872 | tf_op jit(solution)/shard_map/ppermute | solution.py:574
  276.5 26.8 %collective-permute-start.34 = (bf16[2,128,1024]{2,1,0:T(8,128)(2,1)}, bf16[2,128,1024]{2,1,0:T(8,128)(2,1)}, u32[]{:S(2)}, u32[]{:S(2)}) collective-permute-start(bf16[2,128,1024]{2,1,0:T(8,128)(2,1)} %broadcast_select_fusion.15), channel_id=1, source_target_pairs={{0,8},{4,12},{5,13},{1,9},{10,2},{14,6},{15,7},{11,3},{16,24},{20,... | collective-permute-start | bytes 1572872 | tf_op jit(solution)/shard_map/ppermute | solution.py:574
  309.5 26.4 %collective-permute-start.42 = (bf16[4,128,1024]{2,1,0:T(8,128)(2,1)}, bf16[4,128,1024]{2,1,0:T(8,128)(2,1)S(1)}, u32[]{:S(2)}, u32[]{:S(2)}) collective-permute-start(bf16[4,128,1024]{2,1,0:T(8,128)(2,1)} %collective-permute-done.36.rest_1_), channel_id=1, source_target_pairs={{1,2},{2,3},{5,6},{6,7},{9,10},{10,11},{13,14},{14,15},{17,18},{18... | collective-permute-start | bytes 3145736 | tf_op jit(solution)/shard_map/ppermute | solution.py:567
  310.3 40.8 %collective-permute-start.43 = (bf16[4,128,1024]{2,1,0:T(8,128)(2,1)S(1)}, bf16[4,128,1024]{2,1,0:T(8,128)(2,1)S(1)}, u32[]{:S(2)}, u32[]{:S(2)}) collective-permute-start(bf16[4,128,1024]{2,1,0:T(8,128)(2,1)S(1)} %collective-permute-done.37.rest_5_), channel_id=1, source_target_pairs={{1,0},{2,1},{5,4},{6,5},{9,8},{10,9},{13,12},{14,13},{17,16},{18,1... | collective-permute-start | bytes 3145736 | tf_op jit(solution)/shard_map/ppermute | solution.py:567
  320.3 14.2 %collective-permute-start.40 = (bf16[2,128,1024]{2,1,0:T(8,128)(2,1)S(1)}, bf16[2,128,1024]{2,1,0:T(8,128)(2,1)S(1)}, u32[]{:S(2)}, u32[]{:S(2)}) collective-permute-start(bf16[2,128,1024]{2,1,0:T(8,128)(2,1)S(1)} %get-tuple-element.420), channel_id=1, source_target_pairs={{0,8},{4,12},{5,13},{1,9},{10,2},{14,6},{15,7},{11,3},{16,24},{20,... | collective-permute-start | bytes 1572872 | tf_op jit(solution)/shard_map/ppermute | solution.py:574
  353.4 14.4 %collective-permute-start.44 = (bf16[2,128,1024]{2,1,0:T(8,128)(2,1)}, bf16[2,128,1024]{2,1,0:T(8,128)(2,1)}, u32[]{:S(2)}, u32[]{:S(2)}) collective-permute-start(bf16[2,128,1024]{2,1,0:T(8,128)(2,1)} %get-tuple-element.418), channel_id=1, source_target_pairs={{0,4},{5,1},{10,14},{15,11},{16,20},{21,17},{26,30},{31,27}} | collective-permute-start | bytes 1572872 | tf_op jit(solution)/shard_map/ppermute | solution.py:574
  362.0 25.1 %collective-permute-start.48 = (bf16[4,128,1024]{2,1,0:T(8,128)(2,1)S(1)}, bf16[4,128,1024]{2,1,0:T(8,128)(2,1)S(1)}, u32[]{:S(2)}, u32[]{:S(2)}) collective-permute-start(bf16[4,128,1024]{2,1,0:T(8,128)(2,1)S(1)} %collective-permute-done.42.rest_2_), channel_id=1, source_target_pairs={{2,3},{6,7},{10,11},{14,15},{18,19},{22,23},{26,27},{30,31}} | collective-permute-start | bytes 3145736 | tf_op jit(solution)/shard_map/ppermute | solution.py:567
  362.7 25.0 %collective-permute-start.49 = (bf16[4,128,1024]{2,1,0:T(8,128)(2,1)S(1)}, bf16[4,128,1024]{2,1,0:T(8,128)(2,1)S(1)}, u32[]{:S(2)}, u32[]{:S(2)}) collective-permute-start(bf16[4,128,1024]{2,1,0:T(8,128)(2,1)S(1)} %collective-permute-done.43.rest_6_), channel_id=1, source_target_pairs={{1,0},{5,4},{9,8},{13,12},{17,16},{21,20},{25,24},{29,28}} | collective-permute-start | bytes 3145736 | tf_op jit(solution)/shard_map/ppermute | solution.py:567
  380.3 15.5 %collective-permute-start.50 = (bf16[4,128,1024]{2,1,0:T(8,128)(2,1)S(1)}, bf16[4,128,1024]{2,1,0:T(8,128)(2,1)S(1)}, u32[]{:S(2)}, u32[]{:S(2)}) collective-permute-start(bf16[4,128,1024]{2,1,0:T(8,128)(2,1)S(1)} %pad_maximum_fusion.11.rest_8_), channel_id=1, source_target_pairs={{0,16},{16,0},{1,17},{17,1},{2,18},{18,2},{3,19},{19,3},{4,20},{20... | collective-permute-start | bytes 3145736 | tf_op jit(solution)/shard_map/ppermute | solution.py:625
  389.0 37.0 %collective-permute-start.52 = (bf16[4,128,1024]{2,1,0:T(8,128)(2,1)}, bf16[4,128,1024]{2,1,0:T(8,128)(2,1)}, u32[]{:S(2)}, u32[]{:S(2)}) collective-permute-start(bf16[4,128,1024]{2,1,0:T(8,128)(2,1)} %pad_maximum_fusion.13.rest_8_), channel_id=1, source_target_pairs={{0,16},{16,0},{1,17},{17,1},{2,18},{18,2},{3,19},{19,3},{4,20},{20... | collective-permute-start | bytes 3145736 | tf_op jit(solution)/shard_map/ppermute | solution.py:625
  389.3 31.2 %collective-permute-start.53 = (bf16[2,128,1024]{2,1,0:T(8,128)(2,1)S(1)}, bf16[2,128,1024]{2,1,0:T(8,128)(2,1)S(1)}, u32[]{:S(2)}, u32[]{:S(2)}) collective-permute-start(bf16[2,128,1024]{2,1,0:T(8,128)(2,1)S(1)} %get-tuple-element.414), channel_id=1, source_target_pairs={{0,4},{5,1},{10,14},{15,11},{16,20},{21,17},{26,30},{31,27}} | collective-permute-start | bytes 1572872 | tf_op jit(solution)/shard_map/ppermute | solution.py:574
  394.5 26.1 %collective-permute-start.54 = (bf16[2,128,1024]{2,1,0:T(8,128)(2,1)S(1)}, bf16[2,128,1024]{2,1,0:T(8,128)(2,1)S(1)}, u32[]{:S(2)}, u32[]{:S(2)}) collective-permute-start(bf16[2,128,1024]{2,1,0:T(8,128)(2,1)S(1)} %get-tuple-element.413), channel_id=1, source_target_pairs={{0,8},{5,13},{10,2},{15,7},{16,24},{21,29},{26,18},{31,23}} | collective-permute-start | bytes 1572872 | tf_op jit(solution)/shard_map/ppermute | solution.py:574
  421.6 20.7 %collective-permute-start.55 = (bf16[2,128,1024]{2,1,0:T(8,128)(2,1)}, bf16[2,128,1024]{2,1,0:T(8,128)(2,1)S(1)}, u32[]{:S(2)}, u32[]{:S(2)}) collective-permute-start(bf16[2,128,1024]{2,1,0:T(8,128)(2,1)} %get-tuple-element.410), channel_id=1, source_target_pairs={{0,8},{4,12},{5,13},{1,9},{10,2},{14,6},{15,7},{11,3},{16,24},{20,... | collective-permute-start | bytes 1572872 | tf_op jit(solution)/shard_map/ppermute | solution.py:574
  423.0 19.4 %collective-permute-start.56 = (bf16[2,128,1024]{2,1,0:T(8,128)(2,1)}, bf16[2,128,1024]{2,1,0:T(8,128)(2,1)S(1)}, u32[]{:S(2)}, u32[]{:S(2)}) collective-permute-start(bf16[2,128,1024]{2,1,0:T(8,128)(2,1)} %get-tuple-element.409), channel_id=1, source_target_pairs={{0,4},{8,12},{5,1},{13,9},{10,14},{2,6},{15,11},{7,3},{16,20},{24,... | collective-permute-start | bytes 1572872 | tf_op jit(solution)/shard_map/ppermute | solution.py:574
  (40 other events, 991.2 us)
Sparse Core Ops, SparseCore 0:
  41.2 95.4 all-gather.2
